TPU v7x, 512 devices: a whole 4x4x16 slice. The times are simulated.
512 devices in a mesh: dom: 512 (over x, y, z, core).
Axes of the slice: x: 4, y: 4, z: 16, core: 2. Of those that a mesh axis runs over, the one named last changes fastest.
Arguments:
- source: float32 [4, 4, 20, 65536], P(None, None, None, 'dom'), may hold values from -6 to 6
- absorption: float32 [4, 65536], P(None, 'dom'), may hold values from 0.5 to 4
- geometry: float32 [3, 65536], P(None, 'dom'), may hold values from 0.2 to 0.6
- penalty: float32 [4, 65536], P(None, 'dom'), may hold values from 0.5 to 4.5
- face_link: int32 [4, 65536], P(None, 'dom'), may hold values from 0 to 768, as said below
- face_orient: int32 [4, 65536], P(None, 'dom'), may hold values from 0 to 5
- send_index: int32 [512, 8, 32], P('dom'), may hold values from 0 to 512, as said below
- live_count: int32 [512], P('dom'), may hold values from 64 to 128, as said below
- mass_matrix: float32 [20, 20], replicated, as said below
- stiffness: float32 [3, 20, 20], replicated, may hold values from -1.25 to 1.25
Outputs:
- solution: float32 [4, 4, 20, 65536], P(None, None, None, 'dom')
- residual: float32 [4, 4, 20, 65536], P(None, None, None, 'dom')
Inputs may be any that keep to these rules, and one draw needn't show every extreme that they name: `face_link`: values below 512 name a local trace f * 128 + local element; values from 512 name received slot q * 32 + s; the largest value means a boundary face. `send_index`: the value 4 * 128 marks an empty slot. `live_count`: some partition is full in every draw. `mass_matrix`: Symmetric, unit diagonal, off-diagonal entries of magnitude at most 0.04.
All inputs are finite; a program needn't handle non-finite values.
Results may differ from a plain program's by a relative error of at most 0.0003.
Values sent between devices are 32-bit elements; how exact they have to be, the bound alone decides.
A program may use at most 64 MiB of HBM per device.

v0:
```python
import jax
import jax.numpy as jnp
import numpy as np
from jax import lax
from jax.sharding import PartitionSpec as P

REACH = 4
ITERS = 2
SLOTS = 32
PEERS = 8


def from_behind(value, axis, by):
    count = lax.axis_size(axis)
    pairs = [(i, i + by) for i in range(count) if 0 <= i + by < count]
    return lax.ppermute(value, axis, pairs)


def node_tables():
    triangle = [(a, b, 3 - a - b) for a in range(4) for b in range(4 - a)]
    tetra_nodes = [
        (i, j, k, 3 - i - j - k) for i in range(4) for j in range(4 - i) for k in range(4 - i - j)
    ]
    face_index = np.zeros((10, 4), np.int32)
    for t in range(10):
        for f in range(4):
            coords = list(triangle[t])
            coords.insert(f, 0)
            face_index[t, f] = tetra_nodes.index(tuple(coords))
    orders = ((0, 1, 2), (1, 2, 0), (2, 0, 1), (0, 2, 1), (2, 1, 0), (1, 0, 2))
    turned = np.zeros((6, 10), np.int32)
    for o in range(6):
        for t in range(10):
            turned[o, t] = triangle.index(tuple((triangle[t][q] for q in orders[o])))
    lifting = np.zeros((20, 40), np.float32)
    for t in range(10):
        for f in range(4):
            lifting[face_index[t, f], t * 4 + f] = 1.0
    return (face_index, turned, lifting)


def face_traces(field):
    face_index, turned, lifting = node_tables()
    count = field.shape[2]
    picked = field[:, face_index.reshape(-1), :]
    return picked.reshape(field.shape[0], 10, 4 * count)


def pack(traces, send_rows):
    blank = jnp.zeros((traces.shape[0], 10, 1), jnp.float32)
    trace_table = jnp.concatenate([traces, blank], axis=2)
    picked = jnp.take(trace_table, send_rows.reshape(-1), axis=2)
    return picked.reshape(traces.shape[0], 10, send_rows.shape[0], send_rows.shape[1])


def coefficient(absorption):
    scale = jnp.array([1.0, 3.0, 3.0, 3.0], jnp.float32)
    return (absorption[:, None, :] * scale[None, :, None]).reshape(-1, absorption.shape[1])


def local_apply(
    field, received, absorption, geometry, penalty, link, orient, live_mask, mass_matrix, stiffness
):
    face_index, turned, lifting = node_tables()
    chans = field.shape[0]
    count = field.shape[2]
    traces = face_traces(field)
    blank = jnp.zeros((chans, 10, 1), jnp.float32)
    trace_table = jnp.concatenate([traces, received, blank], axis=2)
    width = trace_table.shape[2]
    table_flat = trace_table.reshape(chans, 10 * width)
    turned_rows = jnp.take(jnp.asarray(turned, jnp.int32), orient, axis=0)
    turned_rows = jnp.moveaxis(turned_rows, -1, 0)
    column = turned_rows * width + link[None]
    chosen = jnp.take(table_flat, column.reshape(-1), axis=1).reshape(chans, 10, 4, count)
    own_trace = traces.reshape(chans, 10, 4, count)
    jump_term = (penalty[None, None] * (own_trace - chosen)).reshape(chans, 40, count)
    lift_matrix = jnp.asarray(lifting, jnp.float32)
    contrib = jnp.einsum("nk,ckx->cnx", lift_matrix, jump_term, precision=lax.Precision.HIGHEST)
    massed = jnp.einsum("mn,cnx->cmx", mass_matrix, field, precision=lax.Precision.HIGHEST)
    pieces = field.reshape(4, 4, 20, count)
    flux_terms = jnp.einsum(
        "dmn,gdnx->gdmx", stiffness, pieces[:, 1:], precision=lax.Precision.HIGHEST
    )
    toward = jnp.sum(flux_terms * geometry[None, :, None, :], axis=1)
    backward = jnp.einsum("dnm,gnx->gdmx", stiffness, pieces[:, 0], precision=lax.Precision.HIGHEST)
    backward = backward * geometry[None, :, None, :]
    transport = jnp.concatenate([toward[:, None], -backward], axis=1).reshape(chans, 20, count)
    total = coefficient(absorption)[:, None, :] * massed + transport + contrib
    return live_mask * total


def precondition(res, absorption, penalty, mass_inverse):
    denom = coefficient(absorption) + 0.5 * jnp.sum(penalty, axis=0)[None, :]
    solved = jnp.einsum("mn,cnx->cmx", mass_inverse, res, precision=lax.Precision.HIGHEST)
    return solved / denom[:, None, :]


def inverse_mass(mass_matrix):
    factor = jnp.linalg.cholesky(mass_matrix)
    identity = jnp.eye(mass_matrix.shape[0], dtype=mass_matrix.dtype)
    lower_solved = lax.linalg.triangular_solve(factor, identity, left_side=True, lower=True)
    return lax.linalg.triangular_solve(
        factor, lower_solved, left_side=True, lower=True, transpose_a=True
    )


def peer_offset(p, reach):
    return p + 1 if p < reach else -(p - reach + 1)


def trade_traces(traces, send_rows):
    outgoing = pack(traces, send_rows)
    chans = traces.shape[0]
    kept = []
    for p in range(PEERS):
        kept.append(from_behind(outgoing[:, :, p], "dom", peer_offset(p, REACH)))
    return jnp.stack(kept, axis=2).reshape(chans, 10, PEERS * SLOTS)


def body(
    source,
    absorption,
    geometry,
    penalty,
    face_link,
    face_orient,
    send_index,
    live_count,
    mass_matrix,
    stiffness,
):
    count = source.shape[3]
    chans = source.shape[0] * source.shape[1]
    source_flat = source.reshape(chans, source.shape[2], count)
    live_mask = (jnp.arange(count) < live_count[0]).astype(jnp.float32)
    send_rows = send_index[0]
    mass_inverse = inverse_mass(mass_matrix)
    estimate = jnp.where(live_mask > 0.5, 1.0 + 0.25 * jnp.sum(penalty, axis=0), 0.0)
    upper = lax.pmax(jnp.max(estimate), "dom")
    lower = 0.1 * upper
    centre = (upper + lower) / 2.0
    half_width = (upper - lower) / 2.0
    sigma_one = centre / half_width
    ratio_now = 1.0 / sigma_one
    solution = jnp.zeros_like(source_flat)
    residual = live_mask * source_flat
    direction = precondition(residual, absorption, penalty, mass_inverse) / centre
    for step in range(ITERS):
        solution = solution + direction
        received = trade_traces(face_traces(direction), send_rows)
        residual = residual - local_apply(
            direction,
            received,
            absorption,
            geometry,
            penalty,
            face_link,
            face_orient,
            live_mask,
            mass_matrix,
            stiffness,
        )
        if step < ITERS - 1:
            ratio_new = 1.0 / (2.0 * sigma_one - ratio_now)
            direction = (
                ratio_new * ratio_now * direction
                + 2.0
                * ratio_new
                / half_width
                * precondition(residual, absorption, penalty, mass_inverse)
            )
            ratio_now = ratio_new
    return (solution.reshape(source.shape), residual.reshape(source.shape))


def solution(mesh):
    in_specs = (
        P(None, None, None, "dom"),
        P(None, "dom"),
        P(None, "dom"),
        P(None, "dom"),
        P(None, "dom"),
        P(None, "dom"),
        P("dom", None, None),
        P("dom"),
        P(),
        P(),
    )
    out_specs = (P(None, None, None, "dom"), P(None, None, None, "dom"))
    return jax.shard_map(body, mesh=mesh, in_specs=in_specs, out_specs=out_specs, check_vma=False)
```

profile of v0, /device:TPU:1, one launch (start us, length us, event | category | flops | bytes accessed | tf_op | source)
XLA Modules:
  0.0 292.4 jit_solution(18119141386115680193)
XLA Ops:
  1.4 0.9 copy.97
  4.6 1.8 cholesky.17
  7.7 1.5 custom-call.8
  11.0 111.0 %pmax.7 = f32[]{:T(128)} all-reduce(f32[]{:T(128)} %get-tuple-element.31), channel_id=1, replica_groups=mesh['dom'=512] {'dom'}, use_global_device_ids=true, to_apply=%region_4.5 | all-reduce | flops 1 | bytes 8 | tf_op jit(solution)/shard_map/pmax | solution.py:140
  127.3 3.7 %copy.105 = f32[16,10,512]{1,0,2:T(8,128)} copy(f32[16,10,512]{2,1,0:T(8,128)S(1)} %reshape.213) | data formatting | bytes 655360 | tf_op jit(solution)/shard_map/reshape | solution.py:46
  131.1 4.4 %concatenate.19 = f32[16,10,513]{1,0,2:T(8,128)} pad(f32[16,10,512]{1,0,2:T(8,128)} %copy.105, f32[]{:T(128)} %constant.96.clone.1), padding=0_0x0_0x0_1 | pad | bytes 656004 | tf_op jit(solution)/shard_map/concatenate | solution.py:51
  135.5 4.3 %gather_fusion.2 = f32[256,16,10]{2,1,0:T(8,128)} fusion(f32[16,10,513]{1,0,2:T(8,128)} %concatenate.19, s32[1024]{0:T(1024)S(1)} %get-tuple-element.34), kind=kCustom, calls=%fused_computation.clone | custom fusion | bytes 328704 | tf_op jit(solution)/shard_map/jit(_take)/gather | solution.py:52
  139.8 1.9 broadcast_select_fusion.3
  142.2 3.3 %collective-permute-start = (f32[16,10,32]{2,0,1:T(8,128)S(1)}, f32[16,10,32]{2,0,1:T(8,128)S(1)}, u32[]{:S(2)}, u32[]{:S(2)}) collective-permute-start(f32[16,10,32]{2,0,1:T(8,128)S(1)} %bitcast.222), channel_id=1, source_target_pairs={{0,1},{1,2},{2,3},{3,4},{4,5},{5,6},{6,7},{7,8},{8,9},{9,10},{10,1... | collective-permute-start | bytes 61448 | tf_op jit(solution)/shard_map/ppermute | solution.py:16
  145.8 1.4 collective-permute-start.1
  147.4 2.6 collective-permute-start.2
  150.2 4.3 %collective-permute-start.3 = (f32[16,10,32]{2,0,1:T(8,128)S(1)}, f32[16,10,32]{2,0,1:T(8,128)S(1)}, u32[]{:S(2)}, u32[]{:S(2)}) collective-permute-start(f32[16,10,32]{2,0,1:T(8,128)S(1)} %bitcast.219), channel_id=1, source_target_pairs={{0,4},{1,5},{2,6},{3,7},{4,8},{5,9},{6,10},{7,11},{8,12},{9,13},{1... | collective-permute-start | bytes 61448 | tf_op jit(solution)/shard_map/ppermute | solution.py:16
  154.7 2.6 collective-permute-start.4
  157.3 1.0 gather_fusion.3
  162.0 1.3 collective-permute-start.5
  163.3 1.3 collective-permute-start.6
  164.6 1.5 collective-permute-start.7
  166.2 2.2 collective-permute-done.5
  168.4 2.5 collective-permute-done.6
  170.9 4.5 %collective-permute-done.7 = f32[16,10,32]{2,0,1:T(8,128)S(1)} collective-permute-done((f32[16,10,32]{2,0,1:T(8,128)S(1)}, f32[16,10,32]{2,0,1:T(8,128)S(1)}, u32[]{:S(2)}, u32[]{:S(2)}) %collective-permute-start.7) | collective-permute-done | bytes 20512 | tf_op jit(solution)/shard_map/ppermute | solution.py:16
  176.3 2.9 copy.115
  179.2 19.8 %gather_fusion.4 = f32[5120,16]{1,0:T(8,128)} fusion(f32[16,7690]{0,1:T(8,128)} %copy.115, s32[5120]{0:T(1024)S(1)} %fusion.28), kind=kCustom, calls=%fused_computation.2.clone | custom fusion | bytes 675840 | tf_op jit(solution)/shard_map/jit(_take)/gather | solution.py:75
  199.0 4.2 %broadcast_select_fusion.1 = f32[5120,16]{1,0:T(8,128)S(1)} fusion(f32[5120,16]{1,0:T(8,128)} %gather_fusion.4, pred[5120]{0:T(1024)(128)(4,1)S(1)} %compare_and_fusion), kind=kLoop, calls=%fused_computation.8 | loop fusion | flops 81920 | bytes 660480 | tf_op jit(solution)/shard_map/jit(_take)/select_n | solution.py:75
  204.5 1.4 fusion.11
  205.9 1.8 bitcast_add_fusion.1
  208.1 0.9 fusion.18
  209.8 3.7 %copy.124 = f32[16,10,512]{1,0,2:T(8,128)} copy(f32[16,10,512]{2,1,0:T(8,128)S(1)} %reshape.223) | data formatting | bytes 655360 | tf_op jit(solution)/shard_map/reshape | solution.py:46
  213.6 4.4 %concatenate.22 = f32[16,10,513]{1,0,2:T(8,128)} pad(f32[16,10,512]{1,0,2:T(8,128)} %copy.124, f32[]{:T(128)} %constant.96.clone.1), padding=0_0x0_0x0_1 | pad | bytes 656004 | tf_op jit(solution)/shard_map/concatenate | solution.py:51
  218.0 3.1 %gather_fusion.5 = f32[256,16,10]{2,1,0:T(8,128)S(1)} fusion(f32[16,10,513]{1,0,2:T(8,128)} %concatenate.22, s32[1024]{0:T(1024)} %copy-done.18), kind=kCustom, calls=%fused_computation.3.clone | custom fusion | bytes 328704 | tf_op jit(solution)/shard_map/jit(_take)/gather | solution.py:52
  222.4 2.3 collective-permute-start.8
  225.4 1.6 copy.138
  227.9 5.2 %collective-permute-start.9 = (f32[16,10,32]{2,0,1:T(8,128)}, f32[16,10,32]{2,0,1:T(8,128)S(1)}, u32[]{:S(2)}, u32[]{:S(2)}) collective-permute-start(f32[16,10,32]{2,0,1:T(8,128)} %bitcast.71), channel_id=1, source_target_pairs={{0,2},{1,3},{2,4},{3,5},{4,6},{5,7},{6,8},{7,9},{8,10},{9,11},{10,... | collective-permute-start | bytes 61448 | tf_op jit(solution)/shard_map/ppermute | solution.py:16
  233.1 0.8 copy.183
  233.9 3.5 %collective-permute-start.10 = (f32[16,10,32]{2,0,1:T(8,128)}, f32[16,10,32]{2,0,1:T(8,128)S(1)}, u32[]{:S(2)}, u32[]{:S(2)}) collective-permute-start(f32[16,10,32]{2,0,1:T(8,128)} %bitcast.73), channel_id=1, source_target_pairs={{0,3},{1,4},{2,5},{3,6},{4,7},{5,8},{6,9},{7,10},{8,11},{9,12},{10... | collective-permute-start | bytes 61448 | tf_op jit(solution)/shard_map/ppermute | solution.py:16
  237.6 3.7 %collective-permute-start.11 = (f32[16,10,32]{2,0,1:T(8,128)S(1)}, f32[16,10,32]{2,0,1:T(8,128)S(1)}, u32[]{:S(2)}, u32[]{:S(2)}) collective-permute-start(f32[16,10,32]{2,0,1:T(8,128)S(1)} %bitcast.229), channel_id=1, source_target_pairs={{0,4},{1,5},{2,6},{3,7},{4,8},{5,9},{6,10},{7,11},{8,12},{9,13},{1... | collective-permute-start | bytes 61448 | tf_op jit(solution)/shard_map/ppermute | solution.py:16
  241.5 2.6 collective-permute-start.12
  244.7 1.3 collective-permute-start.13
  246.0 1.3 collective-permute-start.14
  247.3 1.3 collective-permute-start.15
  248.8 3.3 %collective-permute-done.13 = f32[16,10,32]{2,0,1:T(8,128)S(1)} collective-permute-done((f32[16,10,32]{2,0,1:T(8,128)S(1)}, f32[16,10,32]{2,0,1:T(8,128)S(1)}, u32[]{:S(2)}, u32[]{:S(2)}) %collective-permute-start.13) | collective-permute-done | bytes 20512 | tf_op jit(solution)/shard_map/ppermute | solution.py:16
  252.1 3.3 %collective-permute-done.14 = f32[16,10,32]{2,0,1:T(8,128)S(1)} collective-permute-done((f32[16,10,32]{2,0,1:T(8,128)S(1)}, f32[16,10,32]{2,0,1:T(8,128)S(1)}, u32[]{:S(2)}, u32[]{:S(2)}) %collective-permute-start.14) | collective-permute-done | bytes 20512 | tf_op jit(solution)/shard_map/ppermute | solution.py:16
  255.4 4.2 %collective-permute-done.15 = f32[16,10,32]{2,0,1:T(8,128)S(1)} collective-permute-done((f32[16,10,32]{2,0,1:T(8,128)S(1)}, f32[16,10,32]{2,0,1:T(8,128)S(1)}, u32[]{:S(2)}, u32[]{:S(2)}) %collective-permute-start.15) | collective-permute-done | bytes 20512 | tf_op jit(solution)/shard_map/ppermute | solution.py:16
  260.5 2.9 copy.134
  263.4 19.8 %gather_fusion.6 = f32[5120,16]{1,0:T(8,128)} fusion(f32[16,7690]{0,1:T(8,128)} %copy.134, s32[5120]{0:T(1024)S(1)} %copy-done.8), kind=kCustom, calls=%fused_computation.4.clone | custom fusion | bytes 675840 | tf_op jit(solution)/shard_map/jit(_take)/gather | solution.py:75
  283.2 4.2 %broadcast_select_fusion = f32[5120,16]{1,0:T(8,128)S(1)} fusion(f32[5120,16]{1,0:T(8,128)} %gather_fusion.6, pred[5120]{0:T(1024)(128)(4,1)S(1)} %compare_and_fusion), kind=kLoop, calls=%fused_computation.7 | loop fusion | flops 81920 | bytes 660480 | tf_op jit(solution)/shard_map/jit(_take)/select_n | solution.py:75
  287.4 1.4 copy.136
  288.9 1.0 subtract_multiply_fusion
  290.4 1.3 fusion.12
  (153 shorter events, 22.7 us)
Async XLA Ops:
  0.6 157.9 %copy-start = (f32[3,20,20]{2,1,0:T(8,128)S(1)}, f32[3,20,20]{2,1,0:T(8,128)}, u32[]{:S(2)}) copy-start(f32[3,20,20]{2,1,0:T(8,128)} %param.41) | copy-start | bytes 14404
  1.4 138.4 %copy-start.24 = (pred[256]{0:T(512)(128)(4,1)}, pred[256]{0:T(512)(128)(4,1)S(1)}, u32[]{:S(2)}) copy-start(pred[256]{0:T(512)(128)(4,1)S(1)} %compare_and_fusion.2) | copy-start | bytes 772
  3.0 124.1 %copy-start.22 = (f32[128]{0:T(128)}, f32[128]{0:T(128)S(1)}, u32[]{:S(2)}) copy-start(f32[128]{0:T(128)S(1)} %compare_convert_fusion) | copy-start | bytes 1540
  9.6 121.5 %copy-start.17 = (f32[20,20,1]{1,0,2:T(8,128)}, f32[20,20,1]{1,0,2:T(8,128)S(1)}, u32[]{:S(2)}) copy-start(f32[20,20,1]{1,0,2:T(8,128)S(1)} %convolution_bitcast_fusion.4) | copy-start | bytes 4804
  124.1 1.7 copy-start.4
  126.5 4.5 %copy-start.21 = (s32[1024]{0:T(1024)}, s32[1024]{0:T(1024)S(1)}, u32[]{:S(2)}) copy-start(s32[1024]{0:T(1024)S(1)} %pad_clamp_fusion.2) | copy-start | bytes 12292
  131.1 4.4 %copy-start.19 = (s32[4,128]{1,0:T(4,128)S(1)}, s32[4,128]{1,0:T(4,128)}, u32[]{:S(2)}) copy-start(s32[4,128]{1,0:T(4,128)} %param.37) | copy-start | bytes 6148
  135.5 6.3 %copy-start.18 = (s32[1024]{0:T(1024)}, s32[1024]{0:T(1024)S(1)}, u32[]{:S(2)}) copy-start(s32[1024]{0:T(1024)S(1)} %get-tuple-element.34) | copy-start | bytes 12292
  141.8 15.6 %copy-start.1 = (s32[6,10]{1,0:T(8,128)S(1)}, s32[6,10]{1,0:T(8,128)}, u32[]{:S(2)}) copy-start(s32[6,10]{1,0:T(8,128)} %constant.109.clone2.1) | copy-start | bytes 724
  142.0 16.5 %copy-start.26 = (s32[4,128]{1,0:T(4,128)S(1)}, s32[4,128]{1,0:T(4,128)}, u32[]{:S(2)}) copy-start(s32[4,128]{1,0:T(4,128)} %param.36) | copy-start | bytes 6148
  142.0 16.6 %copy-start.15 = (f32[3,128]{1,0:T(4,128)S(1)}, f32[3,128]{1,0:T(4,128)}, u32[]{:S(2)}) copy-start(f32[3,128]{1,0:T(4,128)} %param.34) | copy-start | bytes 4612
  142.2 19.7 %collective-permute-start = (f32[16,10,32]{2,0,1:T(8,128)S(1)}, f32[16,10,32]{2,0,1:T(8,128)S(1)}, u32[]{:S(2)}, u32[]{:S(2)}) collective-permute-start(f32[16,10,32]{2,0,1:T(8,128)S(1)} %bitcast.222), channel_id=1, source_target_pairs={{0,1},{1,2},{2,3},{3,4},{4,5},{5,6},{6,7},{7,8},{8,9},{9,10},{10,1... | collective-permute-start | bytes 61448 | tf_op jit(solution)/shard_map/ppermute | solution.py:16
  145.8 17.5 %collective-permute-start.1 = (f32[16,10,32]{2,0,1:T(8,128)S(1)}, f32[16,10,32]{2,0,1:T(8,128)S(1)}, u32[]{:S(2)}, u32[]{:S(2)}) collective-permute-start(f32[16,10,32]{2,0,1:T(8,128)S(1)} %bitcast.221), channel_id=1, source_target_pairs={{0,2},{1,3},{2,4},{3,5},{4,6},{5,7},{6,8},{7,9},{8,10},{9,11},{10,... | collective-permute-start | bytes 61448 | tf_op jit(solution)/shard_map/ppermute | solution.py:16
  147.4 17.2 %collective-permute-start.2 = (f32[16,10,32]{2,0,1:T(8,128)S(1)}, f32[16,10,32]{2,0,1:T(8,128)S(1)}, u32[]{:S(2)}, u32[]{:S(2)}) collective-permute-start(f32[16,10,32]{2,0,1:T(8,128)S(1)} %bitcast.220), channel_id=1, source_target_pairs={{0,3},{1,4},{2,5},{3,6},{4,7},{5,8},{6,9},{7,10},{8,11},{9,12},{10... | collective-permute-start | bytes 61448 | tf_op jit(solution)/shard_map/ppermute | solution.py:16
  150.2 15.9 %collective-permute-start.3 = (f32[16,10,32]{2,0,1:T(8,128)S(1)}, f32[16,10,32]{2,0,1:T(8,128)S(1)}, u32[]{:S(2)}, u32[]{:S(2)}) collective-permute-start(f32[16,10,32]{2,0,1:T(8,128)S(1)} %bitcast.219), channel_id=1, source_target_pairs={{0,4},{1,5},{2,6},{3,7},{4,8},{5,9},{6,10},{7,11},{8,12},{9,13},{1... | collective-permute-start | bytes 61448 | tf_op jit(solution)/shard_map/ppermute | solution.py:16
  154.7 11.4 %collective-permute-start.4 = (f32[16,10,32]{2,0,1:T(8,128)S(1)}, f32[16,10,32]{2,0,1:T(8,128)S(1)}, u32[]{:S(2)}, u32[]{:S(2)}) collective-permute-start(f32[16,10,32]{2,0,1:T(8,128)S(1)} %bitcast.218), channel_id=1, source_target_pairs={{1,0},{2,1},{3,2},{4,3},{5,4},{6,5},{7,6},{8,7},{9,8},{10,9},{11,1... | collective-permute-start | bytes 61448 | tf_op jit(solution)/shard_map/ppermute | solution.py:16
  158.5 20.7 %copy-start.7 = (s32[5120]{0:T(1024)}, s32[5120]{0:T(1024)S(1)}, u32[]{:S(2)}) copy-start(s32[5120]{0:T(1024)S(1)} %fusion.28) | copy-start | bytes 61444
  161.9 14.1 %copy-start.13 = (f32[769]{0:T(1024)}, f32[769]{0:T(1024)S(1)}, u32[]{:S(2)}) copy-start(f32[769]{0:T(1024)S(1)} %pad.9.clone) | copy-start | bytes 9232
  162.0 6.4 %collective-permute-start.5 = (f32[16,10,32]{2,0,1:T(8,128)}, f32[16,10,32]{2,0,1:T(8,128)S(1)}, u32[]{:S(2)}, u32[]{:S(2)}) collective-permute-start(f32[16,10,32]{2,0,1:T(8,128)} %bitcast.42), channel_id=1, source_target_pairs={{2,0},{3,1},{4,2},{5,3},{6,4},{7,5},{8,6},{9,7},{10,8},{11,9},{12,... | collective-permute-start | bytes 61448 | tf_op jit(solution)/shard_map/ppermute | solution.py:16
  163.3 7.6 %collective-permute-start.6 = (f32[16,10,32]{2,0,1:T(8,128)S(1)}, f32[16,10,32]{2,0,1:T(8,128)S(1)}, u32[]{:S(2)}, u32[]{:S(2)}) collective-permute-start(f32[16,10,32]{2,0,1:T(8,128)S(1)} %bitcast.224), channel_id=1, source_target_pairs={{3,0},{4,1},{5,2},{6,3},{7,4},{8,5},{9,6},{10,7},{11,8},{12,9},{13... | collective-permute-start | bytes 61448 | tf_op jit(solution)/shard_map/ppermute | solution.py:16
  164.6 10.8 %collective-permute-start.7 = (f32[16,10,32]{2,0,1:T(8,128)S(1)}, f32[16,10,32]{2,0,1:T(8,128)S(1)}, u32[]{:S(2)}, u32[]{:S(2)}) collective-permute-start(f32[16,10,32]{2,0,1:T(8,128)S(1)} %bitcast.223), channel_id=1, source_target_pairs={{4,0},{5,1},{6,2},{7,3},{8,4},{9,5},{10,6},{11,7},{12,8},{13,9},{1... | collective-permute-start | bytes 61448 | tf_op jit(solution)/shard_map/ppermute | solution.py:16
  203.2 0.7 copy-start.20
  203.2 0.8 copy-start.11
  203.2 1.2 copy-start.5
  203.9 3.8 %copy-start.16 = (f32[3,128]{1,0:T(4,128)S(1)}, f32[3,128]{1,0:T(4,128)}, u32[]{:S(2)}) copy-start(f32[3,128]{1,0:T(4,128)} %param.34) | copy-start | bytes 4612
  204.0 4.1 %copy-start.9 = (f32[10,4,128]{2,1,0:T(4,128)}, f32[10,4,128]{2,1,0:T(4,128)S(1)}, u32[]{:S(2)}) copy-start(f32[10,4,128]{2,1,0:T(4,128)S(1)} %mul.249) | copy-start | bytes 61444
  205.8 2.2 copy-start.2
  213.6 7.5 %copy-start.25 = (pred[256]{0:T(512)(128)(4,1)S(1)}, pred[256]{0:T(512)(128)(4,1)}, u32[]{:S(2)}) copy-start(pred[256]{0:T(512)(128)(4,1)} %copy-done.24) | copy-start | bytes 772
  221.4 3.3 %copy-start.6 = (f32[4,128,20]{1,2,0:T(8,128)S(1)}, f32[4,128,20]{1,2,0:T(8,128)}, u32[]{:S(2)}) copy-start(f32[4,128,20]{1,2,0:T(8,128)} %fusion.18) | copy-start | bytes 122884
  222.4 22.3 %collective-permute-start.8 = (f32[16,10,32]{2,0,1:T(8,128)}, f32[16,10,32]{2,0,1:T(8,128)S(1)}, u32[]{:S(2)}, u32[]{:S(2)}) collective-permute-start(f32[16,10,32]{2,0,1:T(8,128)} %bitcast.68), channel_id=1, source_target_pairs={{0,1},{1,2},{2,3},{3,4},{4,5},{5,6},{6,7},{7,8},{8,9},{9,10},{10,1... | collective-permute-start | bytes 61448 | tf_op jit(solution)/shard_map/ppermute | solution.py:16
  227.9 18.1 %collective-permute-start.9 = (f32[16,10,32]{2,0,1:T(8,128)}, f32[16,10,32]{2,0,1:T(8,128)S(1)}, u32[]{:S(2)}, u32[]{:S(2)}) collective-permute-start(f32[16,10,32]{2,0,1:T(8,128)} %bitcast.71), channel_id=1, source_target_pairs={{0,2},{1,3},{2,4},{3,5},{4,6},{5,7},{6,8},{7,9},{8,10},{9,11},{10,... | collective-permute-start | bytes 61448 | tf_op jit(solution)/shard_map/ppermute | solution.py:16
  233.9 13.4 %collective-permute-start.10 = (f32[16,10,32]{2,0,1:T(8,128)}, f32[16,10,32]{2,0,1:T(8,128)S(1)}, u32[]{:S(2)}, u32[]{:S(2)}) collective-permute-start(f32[16,10,32]{2,0,1:T(8,128)} %bitcast.73), channel_id=1, source_target_pairs={{0,3},{1,4},{2,5},{3,6},{4,7},{5,8},{6,9},{7,10},{8,11},{9,12},{10... | collective-permute-start | bytes 61448 | tf_op jit(solution)/shard_map/ppermute | solution.py:16
  237.4 22.8 %copy-start.14 = (f32[769]{0:T(1024)S(1)}, f32[769]{0:T(1024)}, u32[]{:S(2)}) copy-start(f32[769]{0:T(1024)} %copy-done.13) | copy-start | bytes 9232
  237.6 11.0 %collective-permute-start.11 = (f32[16,10,32]{2,0,1:T(8,128)S(1)}, f32[16,10,32]{2,0,1:T(8,128)S(1)}, u32[]{:S(2)}, u32[]{:S(2)}) collective-permute-start(f32[16,10,32]{2,0,1:T(8,128)S(1)} %bitcast.229), channel_id=1, source_target_pairs={{0,4},{1,5},{2,6},{3,7},{4,8},{5,9},{6,10},{7,11},{8,12},{9,13},{1... | collective-permute-start | bytes 61448 | tf_op jit(solution)/shard_map/ppermute | solution.py:16
  241.5 7.2 %collective-permute-start.12 = (f32[16,10,32]{2,0,1:T(8,128)S(1)}, f32[16,10,32]{2,0,1:T(8,128)S(1)}, u32[]{:S(2)}, u32[]{:S(2)}) collective-permute-start(f32[16,10,32]{2,0,1:T(8,128)S(1)} %bitcast.228), channel_id=1, source_target_pairs={{1,0},{2,1},{3,2},{4,3},{5,4},{6,5},{7,6},{8,7},{9,8},{10,9},{11,1... | collective-permute-start | bytes 61448 | tf_op jit(solution)/shard_map/ppermute | solution.py:16
  244.7 7.4 %collective-permute-start.13 = (f32[16,10,32]{2,0,1:T(8,128)S(1)}, f32[16,10,32]{2,0,1:T(8,128)S(1)}, u32[]{:S(2)}, u32[]{:S(2)}) collective-permute-start(f32[16,10,32]{2,0,1:T(8,128)S(1)} %bitcast.227), channel_id=1, source_target_pairs={{2,0},{3,1},{4,2},{5,3},{6,4},{7,5},{8,6},{9,7},{10,8},{11,9},{12,... | collective-permute-start | bytes 61448 | tf_op jit(solution)/shard_map/ppermute | solution.py:16
  246.0 9.3 %collective-permute-start.14 = (f32[16,10,32]{2,0,1:T(8,128)S(1)}, f32[16,10,32]{2,0,1:T(8,128)S(1)}, u32[]{:S(2)}, u32[]{:S(2)}) collective-permute-start(f32[16,10,32]{2,0,1:T(8,128)S(1)} %bitcast.226), channel_id=1, source_target_pairs={{3,0},{4,1},{5,2},{6,3},{7,4},{8,5},{9,6},{10,7},{11,8},{12,9},{13... | collective-permute-start | bytes 61448 | tf_op jit(solution)/shard_map/ppermute | solution.py:16
  247.3 12.2 %collective-permute-start.15 = (f32[16,10,32]{2,0,1:T(8,128)S(1)}, f32[16,10,32]{2,0,1:T(8,128)S(1)}, u32[]{:S(2)}, u32[]{:S(2)}) collective-permute-start(f32[16,10,32]{2,0,1:T(8,128)S(1)} %bitcast.225), channel_id=1, source_target_pairs={{4,0},{5,1},{6,2},{7,3},{8,4},{9,5},{10,6},{11,7},{12,8},{13,9},{1... | collective-permute-start | bytes 61448 | tf_op jit(solution)/shard_map/ppermute | solution.py:16
  260.3 3.1 %copy-start.8 = (s32[5120]{0:T(1024)S(1)}, s32[5120]{0:T(1024)}, u32[]{:S(2)}) copy-start(s32[5120]{0:T(1024)} %copy-done.7) | copy-start | bytes 61444
  287.4 1.5 copy-start.10
  287.4 2.5 copy-start.12
  287.4 2.9 %copy-start.3 = (f32[16,20,128]{2,1,0:T(8,128)S(1)}, f32[16,20,128]{2,1,0:T(8,128)}, u32[]{:S(2)}) copy-start(f32[16,20,128]{2,1,0:T(8,128)} %copy-done.2) | copy-start | bytes 491524
  287.4 2.9 %copy-start.23 = (f32[128]{0:T(128)S(1)}, f32[128]{0:T(128)}, u32[]{:S(2)}) copy-start(f32[128]{0:T(128)} %copy-done.22) | copy-start | bytes 1540
where the time goes:
time: 297 us; the launch traced here: 292 us
  blocking collectives  111 us (37%)
  local copies, waits for them, and re-layouts  88.3 us (30%)
  starting transfers between devices  39.4 us (13%)
  other arithmetic  21.5 us (7%)
  waiting for transfers between devices  20.1 us (7%)
  matrix products  7.72 us (3%)
  between operations  4.33 us (1%)
    pmax x1, blocking collectives, body(): upper = lax.pmax(jnp.max(estimate), 'dom')  111 us
    gather x2, local copies, waits for them, and re-layouts, local_apply(): jnp.take(table_flat, column.reshape(-1), axis=1)  39.5 us
    ppermute x16, starting transfers between devices, from_behind(): return lax.ppermute(value, axis, pairs)  39.4 us
    ppermute x16, waiting for transfers between devices, from_behind(): return lax.ppermute(value, axis, pairs)  20.1 us
    unnamed x88, local copies, waits for them, and re-layouts  9.99 us
    concatenate x2, local copies, waits for them, and re-layouts, pack(): trace_table = jnp.concatenate([traces, blank], axis=2)  8.82 us
    select_n x2, other arithmetic, local_apply(): jnp.take(table_flat, column.reshape(-1), axis=1)  8.41 us
    reshape x4, local copies, waits for them, and re-layouts, face_traces(): return picked.reshape(field.shape[0], 10, 4 * count)  7.59 us
  transfers between devices with their start and end apart: 16, of which 7 were waited for; matrix products, arithmetic and copies ran while one was open for 3% of the time, Pallas kernels for 0%

commit v1 on v0

v1 whole, which is shorter than its diff:
```python
import functools

import jax
import jax.numpy as jnp
import numpy as np
from jax import lax
from jax.experimental import pallas as pl
from jax.experimental.pallas import tpu as pltpu
from jax.sharding import PartitionSpec as P

MESH = pl.DeviceIdType.MESH
F32 = jnp.float32
BF16 = jnp.bfloat16
GASES = 4
COMPS = 4
NODES = 20
FACES = 4
TRI = 10
SLOTS = 32
PEERS = 8
LANES = 128
OFFSETS = tuple(q + 1 if q < 4 else -(q - 3) for q in range(PEERS))
LOCAL = FACES * LANES
REMOTE = PEERS * SLOTS
ROWS = 2 * TRI * 8
PART = ROWS // 4
FIELD = NODES * 8


def node_tables():
    triangle = [(a, b, 3 - a - b) for a in range(4) for b in range(4 - a)]
    tetra_nodes = [
        (i, j, k, 3 - i - j - k) for i in range(4) for j in range(4 - i) for k in range(4 - i - j)
    ]
    face_index = np.zeros((10, 4), np.int32)
    for t in range(10):
        for f in range(4):
            coords = list(triangle[t])
            coords.insert(f, 0)
            face_index[t, f] = tetra_nodes.index(tuple(coords))
    orders = ((0, 1, 2), (1, 2, 0), (2, 0, 1), (0, 2, 1), (2, 1, 0), (1, 0, 2))
    turned = np.zeros((6, 10), np.int32)
    for o in range(6):
        for t in range(10):
            turned[o, t] = triangle.index(tuple((triangle[t][q] for q in orders[o])))
    return face_index.tolist(), turned.tolist()


FACE_NODE, TURNED = node_tables()


def radices(count):
    digits = []
    while count > 1:
        digit = 8 if count % 8 == 0 else count
        digits.append(digit)
        count //= digit
    return digits


def iota(shape, axis):
    return lax.broadcasted_iota(jnp.int32, shape, axis)


def split(value):
    high = value.astype(BF16).astype(F32)
    return high, value - high


def dot(a, b):
    return jnp.dot(a, b, preferred_element_type=F32)


def invert(matrix):
    size = matrix.shape[0]
    row_id, col_id = iota((size, size), 0), iota((size, size), 1)
    for k in range(size):
        pivot = 1.0 / matrix[k : k + 1, k : k + 1]
        row = jnp.where(col_id[:1] == k, 1.0, matrix[k : k + 1, :]) * pivot
        col = jnp.where(row_id[:, :1] == k, 0.0, matrix[:, k : k + 1])
        rest = jnp.where(col_id == k, 0.0, matrix) - col * row
        matrix = jnp.where(row_id == k, row, rest)
    return matrix


def spread_rows():
    return (iota((FIELD, NODES), 0) // 8 == iota((FIELD, NODES), 1)).astype(F32).astype(BF16)


def spread_columns():
    shape = (3 * NODES, 3 * FIELD)
    return (iota(shape, 1) // 8 == iota(shape, 0)).astype(F32).astype(BF16)


def thrice(matrix):
    high, low = split(matrix)
    return jnp.concatenate([high, high, low], axis=1).astype(BF16)


def times(weights, field):
    high, low = split(field)
    return dot(weights, jnp.concatenate([high, low, high], axis=0).astype(BF16))


def pair_up(first, second):
    sub = iota(first.shape, 1)
    even = jnp.where(sub < 4, first, pltpu.roll(second, 4, 1))
    odd = jnp.where(sub < 4, pltpu.roll(first, 4, 1), second)
    return even, odd


def kernel(
    n,
    source,
    absorption,
    geometry,
    penalty,
    link,
    orient,
    send_index,
    live_count,
    mass,
    stiffness,
    solution_out,
    residual_out,
    source_v,
    absorption_v,
    geometry_v,
    penalty_v,
    link_v,
    orient_v,
    send_v,
    mass_v,
    stiffness_v,
    rhs,
    direction,
    applied,
    second,
    mass_weights,
    flux_weights,
    pick_send,
    pick_local,
    pick_remote,
    table,
    outgoing,
    incoming,
    best,
    best_in,
    sol_v,
    res_v,
    in_sem,
    out_sem,
    send_sem,
    recv_sem,
    best_send,
    best_recv,
):
    me = lax.axis_index("dom")
    peers = [lax.rem(me + o + n, n) for o in OFFSETS]
    digits = radices(n)
    groups = []
    weight = 1
    for digit in digits:
        mine = lax.rem(me // weight, digit)
        groups.append(
            [me + (lax.rem(mine + k, digit) - mine) * weight for k in range(1, digit)]
        )
        weight *= digit

    barrier = pltpu.get_barrier_semaphore()
    everyone = peers + [d for group in groups for d in group]
    for device in everyone:
        pl.semaphore_signal(barrier, inc=1, device_id=(device,), device_id_type=MESH)

    loads = []
    for i, (src, dst) in enumerate(
        (
            (mass, mass_v),
            (source, source_v),
            (absorption, absorption_v),
            (penalty, penalty_v),
            (send_index, send_v),
            (geometry, geometry_v),
            (link, link_v),
            (orient, orient_v),
            (stiffness, stiffness_v),
        )
    ):
        copy = pltpu.make_async_copy(src, dst, in_sem.at[i])
        copy.start()
        loads.append(copy)
    for copy in loads:
        copy.wait()

    rows = spread_rows()
    columns = spread_columns()
    inverse = thrice(invert(mass_v[...]))
    square = (FIELD, 3 * FIELD)
    lane_of, row_of = iota(square, 1), iota(square, 0)
    wide = dot(dot(rows, inverse).astype(BF16), columns)
    mass_weights[...] = jnp.where(lane_of % 8 == row_of % 8, wide, 0.0).astype(BF16)

    live = (iota((1, LANES), 1) < live_count[0]).astype(F32)
    pen = [penalty_v[f : f + 1, :] for f in range(FACES)]
    pen_sum = pen[0] + pen[1] + pen[2] + pen[3]
    best[0] = jnp.where(live > 0.5, 1.0 + 0.25 * pen_sum, 0.0)
    sub = iota((8, LANES), 0)
    scale = jnp.where(sub % 4 == 0, 1.0, 3.0)
    coef = jnp.concatenate(
        [
            jnp.where(
                sub < 4,
                absorption_v[2 * pair : 2 * pair + 1, :],
                absorption_v[2 * pair + 1 : 2 * pair + 2, :],
            )
            * scale
            for pair in range(2)
        ],
        axis=1,
    )
    pen_sum_two = jnp.concatenate([pen_sum, pen_sum], axis=1)
    live_two = jnp.concatenate([live, live], axis=1)
    inv_denom = 1.0 / (coef + 0.5 * pen_sum_two)
    ratio = coef * inv_denom

    for pair in range(2):
        first = source_v[pl.ds(160 * pair, 80), :].reshape(10, 8, LANES)
        other = source_v[pl.ds(160 * pair + 80, 80), :].reshape(10, 8, LANES)
        even, odd = pair_up(first, other)
        lanes = pl.ds(pair * LANES, LANES)
        for p in range(10):
            rhs[2 * p, :, lanes] = even[p] * live
            rhs[2 * p + 1, :, lanes] = odd[p] * live

    def precondition(value, target):
        solved = times(mass_weights[...], value.reshape(FIELD, 2 * LANES))
        target[...] = solved.reshape(NODES, 8, 2 * LANES) * inv_denom[None]

    def fill_table(field):
        high, low = split(field[...])
        for h, part in enumerate((high, low)):
            for pair in range(2):
                block = jnp.concatenate(
                    [
                        jnp.concatenate(
                            [
                                part[FACE_NODE[t][f], :, pair * LANES : (pair + 1) * LANES]
                                for f in range(FACES)
                            ],
                            axis=1,
                        )
                        for t in range(TRI)
                    ],
                    axis=0,
                )
                table[pl.ds(h * ROWS + pair * 80, 80), :] = block.astype(BF16)

    group_of = iota((PART, LANES), 1) // SLOTS

    def pack(trade):
        both = dot(table[...], pick_send[...])
        packed = both[:ROWS] + both[ROWS:]
        for half in range(2):
            parts = [
                packed[j * PART : (j + 1) * PART, half * LANES : (half + 1) * LANES]
                for j in range(4)
            ]
            for q in range(4):
                message = None
                for j in range(4):
                    shift = (j - q) * SLOTS % LANES
                    part = pltpu.roll(parts[j], shift, 1) if shift else parts[j]
                    message = part if message is None else jnp.where(group_of == j, part, message)
                outgoing[trade, half * 4 + q] = message

    def unpack(trade):
        blocks = []
        for j in range(4):
            halves = []
            for half in range(2):
                gathered = None
                for q in range(4):
                    shift = (q - j) * SLOTS % LANES
                    part = incoming[trade, half * 4 + q]
                    part = pltpu.roll(part, shift, 1) if shift else part
                    gathered = part if gathered is None else jnp.where(group_of == q, part, gathered)
                halves.append(gathered)
            blocks.append(jnp.concatenate(halves, axis=1))
        received = jnp.concatenate(blocks, axis=0)
        high, low = split(received)
        return jnp.concatenate([high, low], axis=0).astype(BF16)

    def trade_copies(trade):
        return [
            pltpu.make_async_remote_copy(
                src_ref=outgoing.at[trade, q],
                dst_ref=incoming.at[trade, q],
                send_sem=send_sem.at[trade, q],
                recv_sem=recv_sem.at[trade, q],
                device_id=(peers[q],),
                device_id_type=MESH,
            )
            for q in range(PEERS)
        ]

    slot_at = []
    total = 0
    for digit in digits:
        slot_at.append(total)
        total += digit - 1

    def best_copies(level):
        return [
            pltpu.make_async_remote_copy(
                src_ref=best.at[level],
                dst_ref=best_in.at[slot_at[level] + k],
                send_sem=best_send.at[slot_at[level] + k],
                recv_sem=best_recv.at[slot_at[level] + k],
                device_id=(device,),
                device_id_type=MESH,
            )
            for k, device in enumerate(groups[level])
        ]

    def best_merge(level, copies):
        value = best[level]
        for k, copy in enumerate(copies):
            copy.wait_recv()
            value = jnp.maximum(value, best_in[slot_at[level] + k])
        best[level + 1] = value

    precondition(rhs[...], direction)

    sends = send_v[0]
    four = jnp.concatenate([sends, sends, sends, sends], axis=1)
    slot_q, slot_lane = iota((PEERS, LANES), 0), iota((PEERS, LANES), 1)
    for half in range(2):
        keep = slot_q == half * 4 + slot_lane // SLOTS
        chosen = jnp.sum(jnp.where(keep, four, 0), axis=0, keepdims=True)
        pick = iota((LOCAL, LANES), 0) == chosen
        pick_send[:, pl.ds(half * LANES, LANES)] = pick.astype(F32).astype(BF16)

    fill_table(direction)
    pack(0)

    pl.semaphore_wait(barrier, len(everyone))
    trades = [trade_copies(0), trade_copies(1)]
    for copy in trades[0]:
        copy.start()
    rounds = [best_copies(level) for level in range(len(digits))]
    for copy in rounds[0]:
        copy.start()

    for f in range(FACES):
        lanes = pl.ds(f * LANES, LANES)
        wanted = link_v[f : f + 1, :]
        pick_local[:, lanes] = (iota((LOCAL, LANES), 0) == wanted).astype(F32).astype(BF16)
        for q in range(PEERS):
            origin = me - OFFSETS[q]
            inside = jnp.logical_and(origin >= 0, origin < n).astype(F32)
            pick = (iota((SLOTS, LANES), 0) + (LOCAL + q * SLOTS) == wanted).astype(F32)
            pick_remote[pl.ds(q * SLOTS, SLOTS), lanes] = (pick * inside).astype(BF16)

    flux = jnp.zeros(square, F32)
    for d in range(3):
        ahead = thrice(stiffness_v[d])
        back = thrice(stiffness_v[d].T)
        from_flux = (row_of % 8) + (d + 1) == lane_of % 8
        from_flux = jnp.logical_and(from_flux, row_of % 4 == 0)
        to_flux = (lane_of % 8) + (d + 1) == row_of % 8
        to_flux = jnp.logical_and(to_flux, lane_of % 4 == 0)
        flux = jnp.where(from_flux, dot(dot(rows, ahead).astype(BF16), columns), flux)
        flux = jnp.where(to_flux, dot(dot(rows, back).astype(BF16), columns), flux)
    flux_weights[...] = flux.astype(BF16)

    geo = jnp.concatenate([geometry_v[d : d + 1, :] for d in range(3)], axis=0)
    geo_in = jnp.where(sub % 4 == 0, 1.0, 0.0)
    geo_out = geo_in
    for d in range(3):
        here = sub % 4 == d + 1
        geo_in = jnp.where(here, geo[d : d + 1], geo_in)
        geo_out = jnp.where(here, -geo[d : d + 1], geo_out)
    geo_in = jnp.concatenate([geo_in, geo_in], axis=1)
    geo_out = jnp.concatenate([geo_out, geo_out], axis=1)

    pen_node = []
    for node in range(NODES):
        value = None
        for t in range(TRI):
            for f in range(FACES):
                if FACE_NODE[t][f] == node:
                    value = pen[f] if value is None else value + pen[f]
        pen_node.append(jnp.concatenate([value, value], axis=1))
    pen_row = jnp.concatenate(pen, axis=1)
    orient_row = jnp.concatenate([orient_v[f : f + 1, :] for f in range(FACES)], axis=1)

    def apply_local(field):
        both = dot(table[...], pick_local[...])
        value = field[...]
        flux_term = times(flux_weights[...], (value * geo_in[None]).reshape(FIELD, 2 * LANES))
        return both[:ROWS] + both[ROWS:], flux_term.reshape(NODES, 8, 2 * LANES)

    def apply_remote(field, solved, local, received, target):
        near, flux_term = local
        both = dot(received, pick_remote[...])
        across = near + both[:ROWS] + both[ROWS:]
        total = [None] * NODES
        for t in range(TRI):
            sides = []
            for pair in range(2):
                def rows_of(node):
                    start = pair * 80 + node * 8
                    return across[start : start + 8]

                side = rows_of(TURNED[0][t])
                for o in range(1, 6):
                    if TURNED[o][t] != TURNED[0][t]:
                        side = jnp.where(orient_row == o, rows_of(TURNED[o][t]), side)
                sides.append(side * pen_row)
            for f in range(FACES):
                lanes = slice(f * LANES, (f + 1) * LANES)
                jump = jnp.concatenate([side[:, lanes] for side in sides], axis=1)
                node = FACE_NODE[t][f]
                total[node] = jump if total[node] is None else total[node] + jump
        for node in range(NODES):
            value = ratio * solved[node] + geo_out * flux_term[node]
            value = value + pen_node[node] * field[node] - total[node]
            target[node] = live_two * value

    local = apply_local(direction)
    best_merge(0, rounds[0])
    if len(digits) > 1:
        for copy in rounds[1]:
            copy.start()
    for copy in trades[0]:
        copy.wait_recv()
    apply_remote(direction, rhs, local, unpack(0), applied)

    precondition(applied[...], second)
    fill_table(second)
    pack(1)
    for copy in trades[1]:
        copy.start()
    if len(digits) > 1:
        best_merge(1, rounds[1])
    if len(digits) > 2:
        for copy in rounds[2]:
            copy.start()
    local = apply_local(second)
    for copy in trades[1]:
        copy.wait_recv()
    twice = sol_v
    apply_remote(second, applied, local, unpack(1), twice)

    for level in range(2, len(digits)):
        best_merge(level, rounds[level])

    upper = jnp.max(best[len(digits)], axis=1, keepdims=True)
    lower = 0.1 * upper
    centre = (upper + lower) / 2.0
    half_width = (upper - lower) / 2.0
    sigma_one = centre / half_width
    ratio_now = 1.0 / sigma_one
    ratio_new = 1.0 / (2.0 * sigma_one - ratio_now)
    inv_centre = 1.0 / centre
    step = 2.0 * ratio_new / half_width
    first_weight = inv_centre + ratio_new * ratio_now * inv_centre + step
    second_weight = -step * inv_centre
    sol = first_weight * direction[...] + second_weight * second[...]
    res = rhs[...] - first_weight * applied[...] - second_weight * twice[...]
    for value, target in ((sol, source_v), (res, res_v)):
        for pair in range(2):
            lanes = slice(pair * LANES, (pair + 1) * LANES)
            for p in range(10):
                even, odd = value[2 * p, :, lanes], value[2 * p + 1, :, lanes]
                low, high = pair_up(even[None], odd[None])
                target[pl.ds(160 * pair + 8 * p, 8), :] = low[0]
                target[pl.ds(160 * pair + 80 + 8 * p, 8), :] = high[0]

    stores = [
        pltpu.make_async_copy(source_v, solution_out, out_sem.at[0]),
        pltpu.make_async_copy(res_v, residual_out, out_sem.at[1]),
    ]
    for copy in stores:
        copy.start()
    for copies in trades + rounds:
        for copy in copies:
            copy.wait_send()
    for copy in stores:
        copy.wait()


def solution(mesh):
    n = mesh.shape["dom"]
    digits = radices(n)
    links = sum(digits) - len(digits)

    def body(
        source, absorption, geometry, penalty, link, orient, send_index, live_count, mass, stiffness
    ):
        flat = source.transpose(0, 2, 1, 3).reshape(GASES * NODES * COMPS, LANES)
        anywhere = pl.BlockSpec(memory_space=pl.ANY)
        vmem = pltpu.VMEM
        outs = pl.pallas_call(
            functools.partial(kernel, n),
            out_shape=[jax.ShapeDtypeStruct(flat.shape, F32)] * 2,
            in_specs=[anywhere] * 7
            + [pl.BlockSpec(memory_space=pltpu.SMEM)]
            + [anywhere] * 2,
            out_specs=[anywhere] * 2,
            scratch_shapes=[
                vmem((320, LANES), F32),
                vmem((4, LANES), F32),
                vmem((3, LANES), F32),
                vmem((4, LANES), F32),
                vmem((4, LANES), jnp.int32),
                vmem((4, LANES), jnp.int32),
                vmem((1, PEERS, SLOTS), jnp.int32),
                vmem((NODES, NODES), F32),
                vmem((3, NODES, NODES), F32),
                vmem((NODES, 8, 2 * LANES), F32),
                vmem((NODES, 8, 2 * LANES), F32),
                vmem((NODES, 8, 2 * LANES), F32),
                vmem((NODES, 8, 2 * LANES), F32),
                vmem((FIELD, 3 * FIELD), BF16),
                vmem((FIELD, 3 * FIELD), BF16),
                vmem((LOCAL, REMOTE), BF16),
                vmem((LOCAL, LOCAL), BF16),
                vmem((REMOTE, LOCAL), BF16),
                vmem((2 * ROWS, LOCAL), BF16),
                vmem((2, PEERS, PART, LANES), F32),
                vmem((2, PEERS, PART, LANES), F32),
                vmem((len(digits) + 1, 1, LANES), F32),
                vmem((links, 1, LANES), F32),
                vmem((NODES, 8, 2 * LANES), F32),
                vmem((320, LANES), F32),
                pltpu.SemaphoreType.DMA((9,)),
                pltpu.SemaphoreType.DMA((2,)),
                pltpu.SemaphoreType.DMA((2, PEERS)),
                pltpu.SemaphoreType.DMA((2, PEERS)),
                pltpu.SemaphoreType.DMA((links,)),
                pltpu.SemaphoreType.DMA((links,)),
            ],
            compiler_params=pltpu.CompilerParams(
                collective_id=0, has_side_effects=True, vmem_limit_bytes=32 * 2**20
            ),
            cost_estimate=pl.CostEstimate(
                flops=2_000_000_000, bytes_accessed=1_000_000, transcendentals=0
            ),
        )(flat, absorption, geometry, penalty, link, orient, send_index, live_count, mass, stiffness)
        return tuple(
            out.reshape(GASES, NODES, COMPS, LANES).transpose(0, 2, 1, 3) for out in outs
        )

    in_specs = (
        P(None, None, None, "dom"),
        P(None, "dom"),
        P(None, "dom"),
        P(None, "dom"),
        P(None, "dom"),
        P(None, "dom"),
        P("dom", None, None),
        P("dom"),
        P(),
        P(),
    )
    out_specs = (P(None, None, None, "dom"), P(None, None, None, "dom"))
    return jax.shard_map(body, mesh=mesh, in_specs=in_specs, out_specs=out_specs, check_vma=False)
```

time: 297 us -> 41.6 us (0.14); the launches traced: 292 us -> 41.2 us
  blocking collectives: 111 us -> 0 us
  local copies, waits for them, and re-layouts: 88.3 us -> 7.15 us
  starting transfers between devices: 39.4 us -> 0 us
  Pallas kernels: 0 us -> 32.8 us
  other arithmetic: 21.5 us -> 0 us
  waiting for transfers between devices: 20.1 us -> 0 us
  matrix products: 7.72 us -> 0 us
  between operations: 4.33 us -> 1.32 us
    pmax x1 -> x0, blocking collectives: 111 us -> none  [body(): upper = lax.pmax(jnp.max(estimate), 'dom')]
    gather x10 -> x0, local copies, waits for them, and re-layouts: 49.6 us -> none  [the longest x2 39.5 us: local_apply(): jnp.take(table_flat, column.reshape(-1), axis=1)]
    ppermute x16 -> x0, starting transfers between devices: 39.4 us -> none  [from_behind(): return lax.ppermute(value, axis, pairs)]
    pallas_call x0 -> x1, Pallas kernels: none -> 32.8 us  [body(): pl.pallas_call(functools.partial(kernel, n), out_shape=[jax.ShapeDtypeStr...]
    ppermute x16 -> x0, waiting for transfers between devices: 20.1 us -> none  [from_behind(): return lax.ppermute(value, axis, pairs)]
    reshape x14 -> x0, local copies, waits for them, and re-layouts: 17.2 us -> none  [the longest x4 7.59 us: face_traces(): return picked.reshape(field.shape[0], 10, 4 * count)]
    select_n x5 -> x0, other arithmetic: 10.7 us -> none  [the longest x2 8.41 us: local_apply(): jnp.take(table_flat, column.reshape(-1), axis=1)]
    concatenate x3 -> x0, local copies, waits for them, and re-layouts: 8.83 us -> none  [the longest x2 8.82 us: pack(): trace_table = jnp.concatenate([traces, blank], axis=2)]
  transfers between devices with their start and end apart: 16 -> 0, of which waited for: 7 -> 0; matrix products, arithmetic and copies ran while one was open for 3% -> 0% of each run, Pallas kernels for 0% -> 0%
where the time goes in v1:
time: 41.6 us; the launch traced here: 41.2 us
  Pallas kernels  32.8 us (79%)
  local copies, waits for them, and re-layouts  7.15 us (17%)
  between operations  1.32 us (3%)
    pallas_call x1, Pallas kernels, body(): pl.pallas_call(functools.partial(kernel, n), out_shape=[jax.ShapeDtypeStr...  32.8 us
    unnamed x20, local copies, waits for them, and re-layouts  7.15 us

profile of v1, /device:TPU:1, one launch (start us, length us, event | category | flops | bytes accessed | tf_op | source)
XLA Modules:
  0.0 41.2 jit_solution(18029975135160945806)
XLA Ops:
  0.6 0.0 copy-start.4
  1.3 0.0 copy-done.4
  1.3 0.0 copy-start
  1.3 0.9 %copy-done = f32[4,4,20,128]{3,1,2,0:T(4,128)S(1)} copy-done((f32[4,4,20,128]{3,1,2,0:T(4,128)S(1)}, f32[4,4,20,128]{3,1,2,0:T(4,128)}, u32[]{:S(2)}) %copy-start) | copy-done | bytes 163864
  2.2 0.0 copy-start.1
  2.2 0.8 %copy-done.1 = f32[3,20,20]{2,1,0:T(8,128)S(1)} copy-done((f32[3,20,20]{2,1,0:T(8,128)S(1)}, f32[3,20,20]{2,1,0:T(8,128)}, u32[]{:S(2)}) %copy-start.1) | copy-done | bytes 4824
  3.0 0.0 copy-start.2
  3.0 0.7 %copy-done.2 = f32[20,20]{1,0:T(8,128)S(1)} copy-done((f32[20,20]{1,0:T(8,128)S(1)}, f32[20,20]{1,0:T(8,128)}, u32[]{:S(2)}) %copy-start.2) | copy-done | bytes 1624
  3.7 0.0 copy-start.3
  3.7 0.7 %copy-done.3 = s32[1,8,32]{2,1,0:T(8,128)S(1)} copy-done((s32[1,8,32]{2,1,0:T(8,128)S(1)}, s32[1,8,32]{2,1,0:T(8,128)}, u32[]{:S(2)}) %copy-start.3) | copy-done | bytes 1048
  4.4 0.0 copy-start.5
  4.4 0.7 %copy-done.5 = f32[3,128]{1,0:T(4,128)S(1)} copy-done((f32[3,128]{1,0:T(4,128)S(1)}, f32[3,128]{1,0:T(4,128)}, u32[]{:S(2)}) %copy-start.5) | copy-done | bytes 1560
  5.1 0.0 copy-start.6
  5.1 0.7 %copy-done.6 = f32[4,128]{1,0:T(4,128)S(1)} copy-done((f32[4,128]{1,0:T(4,128)S(1)}, f32[4,128]{1,0:T(4,128)}, u32[]{:S(2)}) %copy-start.6) | copy-done | bytes 2072
  5.8 0.0 copy-start.7
  5.8 0.7 %copy-done.7 = s32[4,128]{1,0:T(4,128)S(1)} copy-done((s32[4,128]{1,0:T(4,128)S(1)}, s32[4,128]{1,0:T(4,128)}, u32[]{:S(2)}) %copy-start.7) | copy-done | bytes 2072
  6.4 0.0 copy-start.8
  6.4 0.7 %copy-done.8 = s32[4,128]{1,0:T(4,128)S(1)} copy-done((s32[4,128]{1,0:T(4,128)S(1)}, s32[4,128]{1,0:T(4,128)}, u32[]{:S(2)}) %copy-start.8) | copy-done | bytes 2072
  7.1 32.8 %shard_map.113 = (f32[320,128]{1,0:T(8,128)S(1)}, f32[320,128]{1,0:T(8,128)S(1)}) custom-call(f32[320,128]{1,0:T(8,128)S(1)} %bitcast.11, f32[4,128]{1,0:T(4,128)S(1)} %copy-done.4, f32[3,128]{1,0:T(4,128)S(1)} %copy-done.5, f32[4,128]{1,0:T(4,128)S(1)} %copy-done.6, s32[4,128]{1,0:T(4,128)S(1)} %copy-done.7, s32[4,128]{1,0:T(4,128)S(1)} %copy-done.8, ...), custom_call_target="tpu_custom_call" | custom-call | flops 2000000000 | bytes 1000000 | tf_op jit(solution)/shard_map/pallas_call | solution.py:504
  39.9 0.7 %copy.15 = f32[4,4,20,128]{3,1,2,0:T(4,128)} copy(f32[4,4,20,128]{3,1,2,0:T(4,128)S(1)} %bitcast.10) | data formatting | bytes 327680
  40.6 0.7 %copy.16 = f32[4,4,20,128]{3,1,2,0:T(4,128)} copy(f32[4,4,20,128]{3,1,2,0:T(4,128)S(1)} %bitcast.9) | data formatting | bytes 327680
Async XLA Ops:
  0.6 0.7 %copy-start.4 = (f32[4,128]{1,0:T(4,128)S(1)}, f32[4,128]{1,0:T(4,128)}, u32[]{:S(2)}) copy-start(f32[4,128]{1,0:T(4,128)} %absorption.1) | copy-start | bytes 6148
  1.3 0.9 %copy-start = (f32[4,4,20,128]{3,1,2,0:T(4,128)S(1)}, f32[4,4,20,128]{3,1,2,0:T(4,128)}, u32[]{:S(2)}) copy-start(f32[4,4,20,128]{3,1,2,0:T(4,128)} %param.10) | copy-start | bytes 491524
  2.2 0.8 %copy-start.1 = (f32[3,20,20]{2,1,0:T(8,128)S(1)}, f32[3,20,20]{2,1,0:T(8,128)}, u32[]{:S(2)}) copy-start(f32[3,20,20]{2,1,0:T(8,128)} %stiffness.1) | copy-start | bytes 14404
  3.0 0.7 %copy-start.2 = (f32[20,20]{1,0:T(8,128)S(1)}, f32[20,20]{1,0:T(8,128)}, u32[]{:S(2)}) copy-start(f32[20,20]{1,0:T(8,128)} %mass.1) | copy-start | bytes 4804
  3.7 0.7 %copy-start.3 = (s32[1,8,32]{2,1,0:T(8,128)S(1)}, s32[1,8,32]{2,1,0:T(8,128)}, u32[]{:S(2)}) copy-start(s32[1,8,32]{2,1,0:T(8,128)} %send_index.1) | copy-start | bytes 3076
  4.4 0.7 %copy-start.5 = (f32[3,128]{1,0:T(4,128)S(1)}, f32[3,128]{1,0:T(4,128)}, u32[]{:S(2)}) copy-start(f32[3,128]{1,0:T(4,128)} %geometry.1) | copy-start | bytes 4612
  5.1 0.7 %copy-start.6 = (f32[4,128]{1,0:T(4,128)S(1)}, f32[4,128]{1,0:T(4,128)}, u32[]{:S(2)}) copy-start(f32[4,128]{1,0:T(4,128)} %penalty.1) | copy-start | bytes 6148
  5.8 0.7 %copy-start.7 = (s32[4,128]{1,0:T(4,128)S(1)}, s32[4,128]{1,0:T(4,128)}, u32[]{:S(2)}) copy-start(s32[4,128]{1,0:T(4,128)} %link.1) | copy-start | bytes 6148
  6.4 0.7 %copy-start.8 = (s32[4,128]{1,0:T(4,128)S(1)}, s32[4,128]{1,0:T(4,128)}, u32[]{:S(2)}) copy-start(s32[4,128]{1,0:T(4,128)} %orient.1) | copy-start | bytes 6148

commit v2 on v1

--- a/solution.py
+++ b/solution.py
@@ -49,13 +49,15 @@
 FACE_NODE, TURNED = node_tables()
 
 
-def radices(count):
-    digits = []
-    while count > 1:
-        digit = 8 if count % 8 == 0 else count
-        digits.append(digit)
-        count //= digit
-    return digits
+ORDER = (3, 7, 2, 6, 1, 5, 0, 4)
+CUBE = 4
+
+
+def torus(count):
+    chips = count // 2
+    z = 16 if chips >= 256 else min(chips, 4)
+    y = min(4, chips // z)
+    return chips // (z * y), y, z
 
 
 def iota(shape, axis):
@@ -130,12 +132,14 @@
     link_v,
     orient_v,
     send_v,
+    live_v,
     mass_v,
     stiffness_v,
     rhs,
     direction,
     applied,
     second,
+    twice,
     mass_weights,
     flux_weights,
     pick_send,
@@ -144,42 +148,63 @@
     table,
     outgoing,
     incoming,
-    best,
-    best_in,
-    sol_v,
-    res_v,
+    own_best,
+    column_in,
+    along_in,
+    level,
+    top,
     in_sem,
-    out_sem,
     send_sem,
     recv_sem,
-    best_send,
-    best_recv,
+    up_send,
+    up_recv,
+    along_send,
+    along_recv,
+    down_send,
+    down_recv,
 ):
     me = lax.axis_index("dom")
-    peers = [lax.rem(me + o + n, n) for o in OFFSETS]
-    digits = radices(n)
-    groups = []
-    weight = 1
-    for digit in digits:
-        mine = lax.rem(me // weight, digit)
-        groups.append(
-            [me + (lax.rem(mine + k, digit) - mine) * weight for k in range(1, digit)]
-        )
-        weight *= digit
+    size_x, size_y, size_z = torus(n)
+    core = lax.rem(me, 2)
+    at_z = lax.rem(me // 2, size_z)
+    at_y = lax.rem(me // (2 * size_z), size_y)
+    at_x = me // (2 * size_z * size_y)
+
+    def device(x, y, z, c):
+        return ((x * size_y + y) * size_z + z) * 2 + c
+
+    peers = [lax.rem(me + OFFSETS[q] + n, n) for q in ORDER]
+    along_x = [device(lax.rem(at_x + k, size_x), at_y, at_z, core) for k in range(1, size_x)]
+    along_y = [device(at_x, lax.rem(at_y + k, size_y), at_z, core) for k in range(1, size_y)]
+    is_head = at_z == 0
+    is_relay = jnp.logical_and(at_z > 0, lax.rem(at_z, CUBE) == 0)
+    others = [(z, c) for z in range(1, size_z) for c in range(2)]
 
     barrier = pltpu.get_barrier_semaphore()
-    everyone = peers + [d for group in groups for d in group]
-    for device in everyone:
-        pl.semaphore_signal(barrier, inc=1, device_id=(device,), device_id_type=MESH)
+
+    def greet(target):
+        pl.semaphore_signal(barrier, inc=1, device_id=(target,), device_id_type=MESH)
+
+    for target in peers:
+        greet(target)
+
+    @pl.when(is_head)
+    def _():
+        greet(device(at_x, at_y, 0, 1 - core))
+        for target in along_x + along_y:
+            greet(target)
+        for z, c in others:
+            greet(device(at_x, at_y, z, c))
 
     loads = []
     for i, (src, dst) in enumerate(
         (
+            (penalty, penalty_v),
+            (live_count, live_v),
             (mass, mass_v),
+            (send_index, send_v),
             (source, source_v),
             (absorption, absorption_v),
-            (penalty, penalty_v),
-            (send_index, send_v),
             (geometry, geometry_v),
             (link, link_v),
             (orient, orient_v),
@@ -189,7 +214,49 @@
         copy = pltpu.make_async_copy(src, dst, in_sem.at[i])
         copy.start()
         loads.append(copy)
-    for copy in loads:
+
+    for copy in loads[:2]:
+        copy.wait()
+    live = (iota((1, LANES), 1) < live_v[0]).astype(F32)
+    pen = [penalty_v[f : f + 1, :] for f in range(FACES)]
+    pen_sum = pen[0] + pen[1] + pen[2] + pen[3]
+    best = jnp.where(live > 0.5, 1.0 + 0.25 * pen_sum, 0.0)
+    own_best[...] = best
+
+    def remote(src, dst, send, recv, target):
+        return pltpu.make_async_remote_copy(
+            src_ref=src,
+            dst_ref=dst,
+            send_sem=send,
+            recv_sem=recv,
+            device_id=(target,),
+            device_id_type=MESH,
+        )
+
+    mine = at_z * 2 + core
+    up = [
+        remote(
+            own_best,
+            column_in.at[mine],
+            up_send.at[i],
+            up_recv.at[mine],
+            device(at_x, at_y, 0, c),
+        )
+        for i, c in enumerate((1 - core, core))
+    ]
+
+    @pl.when(is_head)
+    def _():
+        pl.semaphore_wait(barrier, PEERS + 1 + len(along_x) + len(along_y))
+        up[0].start()
+
+    @pl.when(jnp.logical_not(is_head))
+    def _():
+        pl.semaphore_wait(barrier, PEERS + 2)
+        up[0].start()
+        up[1].start()
+
+    for copy in loads[2:]:
         copy.wait()
 
     rows = spread_rows()
@@ -200,10 +267,27 @@
     wide = dot(dot(rows, inverse).astype(BF16), columns)
     mass_weights[...] = jnp.where(lane_of % 8 == row_of % 8, wide, 0.0).astype(BF16)
 
-    live = (iota((1, LANES), 1) < live_count[0]).astype(F32)
-    pen = [penalty_v[f : f + 1, :] for f in range(FACES)]
-    pen_sum = pen[0] + pen[1] + pen[2] + pen[3]
-    best[0] = jnp.where(live > 0.5, 1.0 + 0.25 * pen_sum, 0.0)
+    sends = send_v[0]
+    four = jnp.concatenate([sends, sends, sends, sends], axis=1)
+    slot_q, slot_group = iota((PEERS, LANES), 0), iota((PEERS, LANES), 1) // SLOTS
+    for half in range(2):
+        wanted = jnp.zeros((PEERS, LANES), jnp.int32)
+        for g in range(4):
+            wanted = jnp.where(slot_group == g, ORDER[half * 4 + g], wanted)
+        chosen = jnp.sum(jnp.where(slot_q == wanted, four, 0), axis=0, keepdims=True)
+        pick = iota((LOCAL, LANES), 0) == chosen
+        pick_send[half] = pick.astype(F32).astype(BF16)
+
+    for f in range(FACES):
+        lanes = pl.ds(f * LANES, LANES)
+        wanted = link_v[f : f + 1, :]
+        pick_local[:, lanes] = (iota((LOCAL, LANES), 0) == wanted).astype(F32).astype(BF16)
+        for place, q in enumerate(ORDER):
+            origin = me - OFFSETS[q]
+            inside = jnp.logical_and(origin >= 0, origin < n).astype(F32)
+            pick = (iota((SLOTS, LANES), 0) + (LOCAL + q * SLOTS) == wanted).astype(F32)
+            pick_remote[pl.ds(place * SLOTS, SLOTS), lanes] = (pick * inside).astype(BF16)
+
     sub = iota((8, LANES), 0)
     scale = jnp.where(sub % 4 == 0, 1.0, 3.0)
     coef = jnp.concatenate(
@@ -257,109 +341,57 @@
 
     group_of = iota((PART, LANES), 1) // SLOTS
 
-    def pack(trade):
-        both = dot(table[...], pick_send[...])
-        packed = both[:ROWS] + both[ROWS:]
+    def trade_copies(trade):
+        return [
+            remote(
+                outgoing.at[trade, place],
+                incoming.at[trade, place],
+                send_sem.at[trade, place],
+                recv_sem.at[trade, place],
+                peers[place],
+            )
+            for place in range(PEERS)
+        ]
+
+    trades = [trade_copies(0), trade_copies(1)]
+
+    def send_traces(trade):
         for half in range(2):
-            parts = [
-                packed[j * PART : (j + 1) * PART, half * LANES : (half + 1) * LANES]
-                for j in range(4)
-            ]
-            for q in range(4):
+            both = dot(table[...], pick_send[half])
+            packed = both[:ROWS] + both[ROWS:]
+            parts = [packed[j * PART : (j + 1) * PART] for j in range(4)]
+            for g in range(4):
                 message = None
                 for j in range(4):
-                    shift = (j - q) * SLOTS % LANES
+                    shift = (j - g) * SLOTS % LANES
                     part = pltpu.roll(parts[j], shift, 1) if shift else parts[j]
                     message = part if message is None else jnp.where(group_of == j, part, message)
-                outgoing[trade, half * 4 + q] = message
-
-    def unpack(trade):
+                outgoing[trade, half * 4 + g] = message
+            for copy in trades[trade][half * 4 : half * 4 + 4]:
+                copy.start()
+
+    def receive_traces(trade):
+        for copy in trades[trade]:
+            copy.wait_recv()
         blocks = []
         for j in range(4):
             halves = []
             for half in range(2):
                 gathered = None
-                for q in range(4):
-                    shift = (q - j) * SLOTS % LANES
-                    part = incoming[trade, half * 4 + q]
+                for g in range(4):
+                    shift = (g - j) * SLOTS % LANES
+                    part = incoming[trade, half * 4 + g]
                     part = pltpu.roll(part, shift, 1) if shift else part
-                    gathered = part if gathered is None else jnp.where(group_of == q, part, gathered)
+                    gathered = part if gathered is None else jnp.where(group_of == g, part, gathered)
                 halves.append(gathered)
             blocks.append(jnp.concatenate(halves, axis=1))
         received = jnp.concatenate(blocks, axis=0)
         high, low = split(received)
         return jnp.concatenate([high, low], axis=0).astype(BF16)
 
-    def trade_copies(trade):
-        return [
-            pltpu.make_async_remote_copy(
-                src_ref=outgoing.at[trade, q],
-                dst_ref=incoming.at[trade, q],
-                send_sem=send_sem.at[trade, q],
-                recv_sem=recv_sem.at[trade, q],
-                device_id=(peers[q],),
-                device_id_type=MESH,
-            )
-            for q in range(PEERS)
-        ]
-
-    slot_at = []
-    total = 0
-    for digit in digits:
-        slot_at.append(total)
-        total += digit - 1
-
-    def best_copies(level):
-        return [
-            pltpu.make_async_remote_copy(
-                src_ref=best.at[level],
-                dst_ref=best_in.at[slot_at[level] + k],
-                send_sem=best_send.at[slot_at[level] + k],
-                recv_sem=best_recv.at[slot_at[level] + k],
-                device_id=(device,),
-                device_id_type=MESH,
-            )
-            for k, device in enumerate(groups[level])
-        ]
-
-    def best_merge(level, copies):
-        value = best[level]
-        for k, copy in enumerate(copies):
-            copy.wait_recv()
-            value = jnp.maximum(value, best_in[slot_at[level] + k])
-        best[level + 1] = value
-
     precondition(rhs[...], direction)
-
-    sends = send_v[0]
-    four = jnp.concatenate([sends, sends, sends, sends], axis=1)
-    slot_q, slot_lane = iota((PEERS, LANES), 0), iota((PEERS, LANES), 1)
-    for half in range(2):
-        keep = slot_q == half * 4 + slot_lane // SLOTS
-        chosen = jnp.sum(jnp.where(keep, four, 0), axis=0, keepdims=True)
-        pick = iota((LOCAL, LANES), 0) == chosen
-        pick_send[:, pl.ds(half * LANES, LANES)] = pick.astype(F32).astype(BF16)
-
     fill_table(direction)
-    pack(0)
-
-    pl.semaphore_wait(barrier, len(everyone))
-    trades = [trade_copies(0), trade_copies(1)]
-    for copy in trades[0]:
-        copy.start()
-    rounds = [best_copies(level) for level in range(len(digits))]
-    for copy in rounds[0]:
-        copy.start()
-
-    for f in range(FACES):
-        lanes = pl.ds(f * LANES, LANES)
-        wanted = link_v[f : f + 1, :]
-        pick_local[:, lanes] = (iota((LOCAL, LANES), 0) == wanted).astype(F32).astype(BF16)
-        for q in range(PEERS):
-            origin = me - OFFSETS[q]
-            inside = jnp.logical_and(origin >= 0, origin < n).astype(F32)
-            pick = (iota((SLOTS, LANES), 0) + (LOCAL + q * SLOTS) == wanted).astype(F32)
-            pick_remote[pl.ds(q * SLOTS, SLOTS), lanes] = (pick * inside).astype(BF16)
+    send_traces(0)
 
     flux = jnp.zeros(square, F32)
     for d in range(3):
@@ -373,13 +405,12 @@
         flux = jnp.where(to_flux, dot(dot(rows, back).astype(BF16), columns), flux)
     flux_weights[...] = flux.astype(BF16)
 
-    geo = jnp.concatenate([geometry_v[d : d + 1, :] for d in range(3)], axis=0)
     geo_in = jnp.where(sub % 4 == 0, 1.0, 0.0)
     geo_out = geo_in
     for d in range(3):
         here = sub % 4 == d + 1
-        geo_in = jnp.where(here, geo[d : d + 1], geo_in)
-        geo_out = jnp.where(here, -geo[d : d + 1], geo_out)
+        geo_in = jnp.where(here, geometry_v[d : d + 1, :], geo_in)
+        geo_out = jnp.where(here, -geometry_v[d : d + 1, :], geo_out)
     geo_in = jnp.concatenate([geo_in, geo_in], axis=1)
     geo_out = jnp.concatenate([geo_out, geo_out], axis=1)
 
@@ -428,34 +459,73 @@
             target[node] = live_two * value
 
     local = apply_local(direction)
-    best_merge(0, rounds[0])
-    if len(digits) > 1:
-        for copy in rounds[1]:
-            copy.start()
-    for copy in trades[0]:
-        copy.wait_recv()
-    apply_remote(direction, rhs, local, unpack(0), applied)
-
+    apply_remote(direction, rhs, local, receive_traces(0), applied)
     precondition(applied[...], second)
     fill_table(second)
-    pack(1)
-    for copy in trades[1]:
-        copy.start()
-    if len(digits) > 1:
-        best_merge(1, rounds[1])
-    if len(digits) > 2:
-        for copy in rounds[2]:
+    send_traces(1)
+    local = apply_local(second)
+
+    def agree(value, first_slot, targets, slot):
+        level[slot] = value
+        copies = [
+            remote(
+                level.at[slot],
+                along_in.at[first_slot + k],
+                along_send.at[first_slot + k],
+                along_recv.at[first_slot + k],
+                target,
+            )
+            for k, target in enumerate(targets)
+        ]
+        for copy in copies:
             copy.start()
-    local = apply_local(second)
-    for copy in trades[1]:
-        copy.wait_recv()
-    twice = sol_v
-    apply_remote(second, applied, local, unpack(1), twice)
-
-    for level in range(2, len(digits)):
-        best_merge(level, rounds[level])
-
-    upper = jnp.max(best[len(digits)], axis=1, keepdims=True)
+        for k, copy in enumerate(copies):
+            copy.wait_recv()
+            value = jnp.maximum(value, along_in[first_slot + k])
+        return value, copies
+
+    down_to = [z for z in (1, 8, 12, 4, 2, 3) if z < size_z]
+    down = [
+        remote(top, top, down_send.at[i], down_recv.at[0], device(at_x, at_y, z, core))
+        for i, z in enumerate(down_to)
+    ]
+    relays = [
+        remote(top, top, down_send.at[i], down_recv.at[0], device(at_x, at_y, at_z + i + 1, core))
+        for i in range(CUBE - 1)
+    ]
+
+    def column_slot(slot):
+        return remote(own_best, column_in.at[slot], up_send.at[0], up_recv.at[slot], peers[0])
+
+    @pl.when(is_head)
+    def _():
+        value = own_best[...]
+        for slot in [1 - core] + [2 * z + c for z, c in others]:
+            column_slot(slot).wait_recv()
+            value = jnp.maximum(value, column_in[slot])
+        value, first = agree(value, 0, along_x, 0)
+        value, then = agree(value, len(along_x), along_y, 1)
+        top[...] = value
+        for copy in down:
+            copy.start()
+        for copy in first + then:
+            copy.wait_send()
+        up[0].wait_send()
+
+    apply_remote(second, applied, local, receive_traces(1), twice)
+
+    @pl.when(jnp.logical_not(is_head))
+    def _():
+        down[0].wait_recv()
+        up[0].wait_send()
+        up[1].wait_send()
+
+    @pl.when(is_relay)
+    def _():
+        for copy in relays:
+            copy.start()
+
+    upper = jnp.max(top[...], axis=1, keepdims=True)
     lower = 0.1 * upper
     centre = (upper + lower) / 2.0
     half_width = (upper - lower) / 2.0
@@ -468,7 +538,7 @@
     second_weight = -step * inv_centre
     sol = first_weight * direction[...] + second_weight * second[...]
     res = rhs[...] - first_weight * applied[...] - second_weight * twice[...]
-    for value, target in ((sol, source_v), (res, res_v)):
+    for value, target in ((sol, solution_out), (res, residual_out)):
         for pair in range(2):
             lanes = slice(pair * LANES, (pair + 1) * LANES)
             for p in range(10):
@@ -477,37 +547,50 @@
                 target[pl.ds(160 * pair + 8 * p, 8), :] = low[0]
                 target[pl.ds(160 * pair + 80 + 8 * p, 8), :] = high[0]
 
-    stores = [
-        pltpu.make_async_copy(source_v, solution_out, out_sem.at[0]),
-        pltpu.make_async_copy(res_v, residual_out, out_sem.at[1]),
-    ]
-    for copy in stores:
-        copy.start()
-    for copies in trades + rounds:
+    for copies in trades:
         for copy in copies:
             copy.wait_send()
-    for copy in stores:
-        copy.wait()
+
+    @pl.when(is_head)
+    def _():
+        for copy in down:
+            copy.wait_send()
+
+    @pl.when(is_relay)
+    def _():
+        for copy in relays:
+            copy.wait_send()
 
 
 def solution(mesh):
     n = mesh.shape["dom"]
-    digits = radices(n)
-    links = sum(digits) - len(digits)
+    size_x, size_y, size_z = torus(n)
+    along = max(size_x + size_y - 2, 1)
 
     def body(
         source, absorption, geometry, penalty, link, orient, send_index, live_count, mass, stiffness
     ):
         flat = source.transpose(0, 2, 1, 3).reshape(GASES * NODES * COMPS, LANES)
-        anywhere = pl.BlockSpec(memory_space=pl.ANY)
+        operands = (
+            flat,
+            absorption,
+            geometry,
+            penalty,
+            link,
+            orient,
+            send_index,
+            live_count,
+            mass,
+            stiffness,
+        )
         vmem = pltpu.VMEM
+        field = vmem((NODES, 8, 2 * LANES), F32)
+        dma = pltpu.SemaphoreType.DMA
         outs = pl.pallas_call(
             functools.partial(kernel, n),
             out_shape=[jax.ShapeDtypeStruct(flat.shape, F32)] * 2,
-            in_specs=[anywhere] * 7
-            + [pl.BlockSpec(memory_space=pltpu.SMEM)]
-            + [anywhere] * 2,
-            out_specs=[anywhere] * 2,
+            in_specs=[pl.BlockSpec(memory_space=pltpu.HBM)] * 10,
+            out_specs=[pl.BlockSpec(memory_space=vmem)] * 2,
             scratch_shapes=[
                 vmem((320, LANES), F32),
                 vmem((4, LANES), F32),
@@ -516,30 +599,36 @@
                 vmem((4, LANES), jnp.int32),
                 vmem((4, LANES), jnp.int32),
                 vmem((1, PEERS, SLOTS), jnp.int32),
+                pltpu.SMEM((1,), jnp.int32),
                 vmem((NODES, NODES), F32),
                 vmem((3, NODES, NODES), F32),
-                vmem((NODES, 8, 2 * LANES), F32),
-                vmem((NODES, 8, 2 * LANES), F32),
-                vmem((NODES, 8, 2 * LANES), F32),
-                vmem((NODES, 8, 2 * LANES), F32),
+                field,
+                field,
+                field,
+                field,
+                field,
                 vmem((FIELD, 3 * FIELD), BF16),
                 vmem((FIELD, 3 * FIELD), BF16),
-                vmem((LOCAL, REMOTE), BF16),
+                vmem((2, LOCAL, LANES), BF16),
                 vmem((LOCAL, LOCAL), BF16),
                 vmem((REMOTE, LOCAL), BF16),
                 vmem((2 * ROWS, LOCAL), BF16),
                 vmem((2, PEERS, PART, LANES), F32),
                 vmem((2, PEERS, PART, LANES), F32),
-                vmem((len(digits) + 1, 1, LANES), F32),
-                vmem((links, 1, LANES), F32),
-                vmem((NODES, 8, 2 * LANES), F32),
-                vmem((320, LANES), F32),
-                pltpu.SemaphoreType.DMA((9,)),
-                pltpu.SemaphoreType.DMA((2,)),
-                pltpu.SemaphoreType.DMA((2, PEERS)),
-                pltpu.SemaphoreType.DMA((2, PEERS)),
-                pltpu.SemaphoreType.DMA((links,)),
-                pltpu.SemaphoreType.DMA((links,)),
+                vmem((1, LANES), F32),
+                vmem((2 * size_z, 1, LANES), F32),
+                vmem((along, 1, LANES), F32),
+                vmem((2, 1, LANES), F32),
+                vmem((1, LANES), F32),
+                dma((10,)),
+                dma((2, PEERS)),
+                dma((2, PEERS)),
+                dma((2,)),
+                dma((2 * size_z,)),
+                dma((along,)),
+                dma((along,)),
+                dma((6,)),
+                dma((1,)),
             ],
             compiler_params=pltpu.CompilerParams(
                 collective_id=0, has_side_effects=True, vmem_limit_bytes=32 * 2**20
@@ -547,7 +636,11 @@
             cost_estimate=pl.CostEstimate(
                 flops=2_000_000_000, bytes_accessed=1_000_000, transcendentals=0
             ),
-        )(flat, absorption, geometry, penalty, link, orient, send_index, live_count, mass, stiffness)
+        )(*[
+                value if value is live_count else pltpu.with_memory_space_constraint(value, pltpu.HBM)
+                for value in operands
+            ]
+        )
         return tuple(
             out.reshape(GASES, NODES, COMPS, LANES).transpose(0, 2, 1, 3) for out in outs
         )

time: 41.6 us -> 37.2 us (0.89)
  local copies, waits for them, and re-layouts: 7.15 us -> 1.33 us
  Pallas kernels: 32.8 us -> 34.4 us
    unnamed x20 -> x2, local copies, waits for them, and re-layouts: 7.15 us -> 1.33 us
    pallas_call x1, Pallas kernels: 32.8 us -> 34.4 us  [body(): pl.pallas_call(functools.partial(kernel, n), out_shape=[jax.ShapeDtypeStr...]
where the time goes in v2:
time: 37.2 us; the launch traced here: 37 us
  Pallas kernels  34.4 us (92%)
  local copies, waits for them, and re-layouts  1.33 us (4%)
  between operations  1.29 us (3%)
    pallas_call x1, Pallas kernels, body(): pl.pallas_call(functools.partial(kernel, n), out_shape=[jax.ShapeDtypeStr...  34.4 us
    unnamed x2, local copies, waits for them, and re-layouts  1.33 us

profile of v2, /device:TPU:1, one launch (start us, length us, event | category | flops | bytes accessed | tf_op | source)
XLA Modules:
  0.0 37.0 jit_solution(10649316854492103121)
XLA Ops:
  1.3 34.4 %shard_map.113 = (f32[320,128]{1,0:T(8,128)S(1)}, f32[320,128]{1,0:T(8,128)S(1)}) custom-call(f32[320,128]{1,0:T(8,128)} %bitcast.11, f32[4,128]{1,0:T(4,128)} %absorption.1, f32[3,128]{1,0:T(4,128)} %geometry.1, f32[4,128]{1,0:T(4,128)} %penalty.1, s32[4,128]{1,0:T(4,128)} %link.1, s32[4,128]{1,0:T(4,128)} %orient.1, s32[1,8,32]{2,1,0:T(8,128)} %send_index.1, ...), custom_call_target="tpu_custom_call" | custom-call | flops 2000000000 | bytes 1000000 | tf_op jit(solution)/shard_map/pallas_call | solution.py:589
  35.7 0.7 %copy.15 = f32[4,4,20,128]{3,1,2,0:T(4,128)} copy(f32[4,4,20,128]{3,1,2,0:T(4,128)S(1)} %bitcast.10) | data formatting | bytes 327680
  36.4 0.7 %copy.16 = f32[4,4,20,128]{3,1,2,0:T(4,128)} copy(f32[4,4,20,128]{3,1,2,0:T(4,128)S(1)} %bitcast.9) | data formatting | bytes 327680

commit v3 on v2

--- a/solution.py
+++ b/solution.py
@@ -51,6 +51,8 @@
 
 ORDER = (3, 7, 2, 6, 1, 5, 0, 4)
 CUBE = 4
+DOWN = {0: (12, 1, 2, 3), 4: (8, 5, 6, 7)}
+EARLY = 4
 
 
 def torus(count):
@@ -75,14 +77,22 @@
 
 def invert(matrix):
     size = matrix.shape[0]
-    row_id, col_id = iota((size, size), 0), iota((size, size), 1)
+    lane, sub = iota((size, LANES), 1), iota((size, LANES), 0)
+    planes = [jnp.broadcast_to(matrix[:, i : i + 1], (size, LANES)) for i in range(size)]
+    state = jnp.stack(planes, axis=0)
     for k in range(size):
-        pivot = 1.0 / matrix[k : k + 1, k : k + 1]
-        row = jnp.where(col_id[:1] == k, 1.0, matrix[k : k + 1, :]) * pivot
-        col = jnp.where(row_id[:, :1] == k, 0.0, matrix[:, k : k + 1])
-        rest = jnp.where(col_id == k, 0.0, matrix) - col * row
-        matrix = jnp.where(row_id == k, row, rest)
-    return matrix
+        pivot = 1.0 / state[k, k : k + 1]
+        row = state[k] * pivot
+        change = jnp.where(sub == k, 1.0 + pivot, row)
+        row = jnp.where(sub == k, pivot, row)
+        rest = state - state[:, k : k + 1, :] * change[None]
+        state = jnp.concatenate(
+            [part for part in (rest[:k], row[None], rest[k + 1 :]) if part.shape[0]], axis=0
+        )
+    inverse = state[0]
+    for i in range(1, size):
+        inverse = jnp.where(lane == i, state[i], inverse)
+    return inverse[:, :size]
 
 
 def spread_rows():
@@ -173,28 +183,34 @@
     def device(x, y, z, c):
         return ((x * size_y + y) * size_z + z) * 2 + c
 
-    peers = [lax.rem(me + OFFSETS[q] + n, n) for q in ORDER]
+    def inside(index):
+        return jnp.logical_and(index >= 0, index < n)
+
+    targets = [me + OFFSETS[q] for q in ORDER]
+    origins = [me - OFFSETS[q] for q in ORDER]
     along_x = [device(lax.rem(at_x + k, size_x), at_y, at_z, core) for k in range(1, size_x)]
     along_y = [device(at_x, lax.rem(at_y + k, size_y), at_z, core) for k in range(1, size_y)]
-    is_head = at_z == 0
-    is_relay = jnp.logical_and(at_z > 0, lax.rem(at_z, CUBE) == 0)
-    others = [(z, c) for z in range(1, size_z) for c in range(2)]
+    planes = [z for z in DOWN if z < size_z]
+    is_head = functools.reduce(jnp.logical_or, [at_z == z for z in planes])
+    is_relay = jnp.logical_and(lax.rem(at_z, CUBE) == 0, jnp.logical_not(is_head))
+    is_early = at_z < EARLY
 
     barrier = pltpu.get_barrier_semaphore()
 
     def greet(target):
         pl.semaphore_signal(barrier, inc=1, device_id=(target,), device_id_type=MESH)
 
-    for target in peers:
-        greet(target)
+    for target in targets:
+        pl.when(inside(target))(functools.partial(greet, target))
 
     @pl.when(is_head)
     def _():
-        greet(device(at_x, at_y, 0, 1 - core))
+        greet(device(at_x, at_y, at_z, 1 - core))
         for target in along_x + along_y:
             greet(target)
-        for z, c in others:
-            greet(device(at_x, at_y, z, c))
+        for k in range(1, size_z):
+            for c in range(2):
+                greet(device(at_x, at_y, lax.rem(at_z + k, size_z), c))
 
     loads = []
     for i, (src, dst) in enumerate(
@@ -238,23 +254,24 @@
         remote(
             own_best,
             column_in.at[mine],
-            up_send.at[i],
+            up_send.at[2 * i + c],
             up_recv.at[mine],
-            device(at_x, at_y, 0, c),
+            device(at_x, at_y, z, c),
         )
-        for i, c in enumerate((1 - core, core))
+        for i, z in enumerate(planes)
+        for c in range(2)
     ]
-
-    @pl.when(is_head)
-    def _():
-        pl.semaphore_wait(barrier, PEERS + 1 + len(along_x) + len(along_y))
-        up[0].start()
-
-    @pl.when(jnp.logical_not(is_head))
-    def _():
-        pl.semaphore_wait(barrier, PEERS + 2)
-        up[0].start()
-        up[1].start()
+    up_to = [jnp.logical_not(jnp.logical_and(at_z == z, core == c)) for z in planes for c in range(2)]
+    partners = sum([inside(target).astype(jnp.int32) for target in targets])
+    partners = partners + sum([wanted.astype(jnp.int32) for wanted in up_to])
+    partners = partners + is_head.astype(jnp.int32) * (len(along_x) + len(along_y))
+
+    def send_up():
+        pl.semaphore_wait(barrier, partners)
+        for wanted, copy in zip(up_to, up):
+            pl.when(wanted)(copy.start)
+
+    pl.when(jnp.logical_not(is_early))(send_up)
 
     for copy in loads[2:]:
         copy.wait()
@@ -283,10 +300,15 @@
         wanted = link_v[f : f + 1, :]
         pick_local[:, lanes] = (iota((LOCAL, LANES), 0) == wanted).astype(F32).astype(BF16)
         for place, q in enumerate(ORDER):
-            origin = me - OFFSETS[q]
-            inside = jnp.logical_and(origin >= 0, origin < n).astype(F32)
-            pick = (iota((SLOTS, LANES), 0) + (LOCAL + q * SLOTS) == wanted).astype(F32)
-            pick_remote[pl.ds(place * SLOTS, SLOTS), lanes] = (pick * inside).astype(BF16)
+            pick = iota((SLOTS, LANES), 0) + (LOCAL + q * SLOTS) == wanted
+            pick_remote[pl.ds(place * SLOTS, SLOTS), lanes] = pick.astype(F32).astype(BF16)
+
+    for place, origin in enumerate(origins):
+
+        @pl.when(jnp.logical_not(inside(origin)))
+        def _(place=place):
+            for trade in range(2):
+                incoming[trade, place] = jnp.zeros((PART, LANES), F32)
 
     sub = iota((8, LANES), 0)
     scale = jnp.where(sub % 4 == 0, 1.0, 3.0)
@@ -348,7 +370,7 @@
                 incoming.at[trade, place],
                 send_sem.at[trade, place],
                 recv_sem.at[trade, place],
-                peers[place],
+                targets[place],
             )
             for place in range(PEERS)
         ]
@@ -367,12 +389,12 @@
                     part = pltpu.roll(parts[j], shift, 1) if shift else parts[j]
                     message = part if message is None else jnp.where(group_of == j, part, message)
                 outgoing[trade, half * 4 + g] = message
-            for copy in trades[trade][half * 4 : half * 4 + 4]:
-                copy.start()
+            for place in range(half * 4, half * 4 + 4):
+                pl.when(inside(targets[place]))(trades[trade][place].start)
 
     def receive_traces(trade):
-        for copy in trades[trade]:
-            copy.wait_recv()
+        for place, copy in enumerate(trades[trade]):
+            pl.when(inside(origins[place]))(copy.wait_recv)
         blocks = []
         for j in range(4):
             halves = []
@@ -391,6 +413,7 @@
 
     precondition(rhs[...], direction)
     fill_table(direction)
+    pl.when(is_early)(send_up)
     send_traces(0)
 
     flux = jnp.zeros(square, F32)
@@ -458,67 +481,76 @@
             value = value + pen_node[node] * field[node] - total[node]
             target[node] = live_two * value
 
+    across = [
+        [
+            remote(
+                level.at[step],
+                along_in.at[first + k],
+                along_send.at[first + k],
+                along_recv.at[first + k],
+                target,
+            )
+            for k, target in enumerate(line)
+        ]
+        for step, (first, line) in enumerate(((0, along_x), (len(along_x), along_y)))
+    ]
+    down = {
+        z: [
+            remote(top, top, down_send.at[i], down_recv.at[0], device(at_x, at_y, to, core))
+            for i, to in enumerate(to for to in DOWN[z] if to < size_z)
+        ]
+        for z in planes
+    }
+    relays = [
+        remote(top, top, down_send.at[i], down_recv.at[0], device(at_x, at_y, at_z + i + 1, core))
+        for i in range(CUBE - 1)
+    ]
+
+    def column_slot(slot):
+        return remote(own_best, column_in.at[slot], up_send.at[0], up_recv.at[slot], me + 1 - 2 * core)
+
+    def meet_column():
+        column_in[mine] = own_best[...]
+        for k in range(1, size_z):
+            for c in range(2):
+                column_slot(lax.rem(at_z + k, size_z) * 2 + c).wait_recv()
+        column_slot(at_z * 2 + 1 - core).wait_recv()
+        level[0] = jnp.max(column_in[...], axis=0)
+        for copy in across[0]:
+            copy.start()
+
+    def meet_line(step, first):
+        value = level[step]
+        for k, copy in enumerate(across[step]):
+            copy.wait_recv()
+            value = jnp.maximum(value, along_in[first + k])
+        return value
+
+    def meet_x():
+        level[1] = meet_line(0, 0)
+        for copy in across[1]:
+            copy.start()
+
+    def meet_y():
+        top[...] = meet_line(1, len(along_x))
+        for z in planes:
+
+            @pl.when(at_z == z)
+            def _(z=z):
+                for copy in down[z]:
+                    copy.start()
+
     local = apply_local(direction)
+    pl.when(is_head)(meet_column)
     apply_remote(direction, rhs, local, receive_traces(0), applied)
     precondition(applied[...], second)
     fill_table(second)
     send_traces(1)
+    pl.when(is_head)(meet_x)
     local = apply_local(second)
-
-    def agree(value, first_slot, targets, slot):
-        level[slot] = value
-        copies = [
-            remote(
-                level.at[slot],
-                along_in.at[first_slot + k],
-                along_send.at[first_slot + k],
-                along_recv.at[first_slot + k],
-                target,
-            )
-            for k, target in enumerate(targets)
-        ]
-        for copy in copies:
-            copy.start()
-        for k, copy in enumerate(copies):
-            copy.wait_recv()
-            value = jnp.maximum(value, along_in[first_slot + k])
-        return value, copies
-
-    down_to = [z for z in (1, 8, 12, 4, 2, 3) if z < size_z]
-    down = [
-        remote(top, top, down_send.at[i], down_recv.at[0], device(at_x, at_y, z, core))
-        for i, z in enumerate(down_to)
-    ]
-    relays = [
-        remote(top, top, down_send.at[i], down_recv.at[0], device(at_x, at_y, at_z + i + 1, core))
-        for i in range(CUBE - 1)
-    ]
-
-    def column_slot(slot):
-        return remote(own_best, column_in.at[slot], up_send.at[0], up_recv.at[slot], peers[0])
-
-    @pl.when(is_head)
-    def _():
-        value = own_best[...]
-        for slot in [1 - core] + [2 * z + c for z, c in others]:
-            column_slot(slot).wait_recv()
-            value = jnp.maximum(value, column_in[slot])
-        value, first = agree(value, 0, along_x, 0)
-        value, then = agree(value, len(along_x), along_y, 1)
-        top[...] = value
-        for copy in down:
-            copy.start()
-        for copy in first + then:
-            copy.wait_send()
-        up[0].wait_send()
-
+    pl.when(is_head)(meet_y)
     apply_remote(second, applied, local, receive_traces(1), twice)
-
-    @pl.when(jnp.logical_not(is_head))
-    def _():
-        down[0].wait_recv()
-        up[0].wait_send()
-        up[1].wait_send()
+    pl.when(jnp.logical_not(is_head))(down[0][0].wait_recv)
 
     @pl.when(is_relay)
     def _():
@@ -548,13 +580,22 @@
                 target[pl.ds(160 * pair + 80 + 8 * p, 8), :] = high[0]
 
     for copies in trades:
-        for copy in copies:
-            copy.wait_send()
+        for place, copy in enumerate(copies):
+            pl.when(inside(targets[place]))(copy.wait_send)
+    for wanted, copy in zip(up_to, up):
+        pl.when(wanted)(copy.wait_send)
 
     @pl.when(is_head)
     def _():
-        for copy in down:
+        for copy in across[0] + across[1]:
             copy.wait_send()
+
+    for z in planes:
+
+        @pl.when(at_z == z)
+        def _(z=z):
+            for copy in down[z]:
+                copy.wait_send()
 
     @pl.when(is_relay)
     def _():
@@ -623,7 +664,7 @@
                 dma((10,)),
                 dma((2, PEERS)),
                 dma((2, PEERS)),
-                dma((2,)),
+                dma((2 * len(DOWN),)),
                 dma((2 * size_z,)),
                 dma((along,)),
                 dma((along,)),

time: 37.2 us -> 32.4 us (0.87)
  the two profiles are of different devices: /device:TPU:1 before, /device:TPU:32 now
where the time goes in v3:
time: 32.4 us; the launch traced here: 32.2 us
  Pallas kernels  29.6 us (91%)
  local copies, waits for them, and re-layouts  1.33 us (4%)
  between operations  1.29 us (4%)
    pallas_call x1, Pallas kernels, body(): pl.pallas_call(functools.partial(kernel, n), out_shape=[jax.ShapeDtypeStr...  29.6 us
    unnamed x2, local copies, waits for them, and re-layouts  1.33 us

profile of v3, /device:TPU:32, one launch (start us, length us, event | category | flops | bytes accessed | tf_op | source)
XLA Modules:
  0.0 32.2 jit_solution(7810513826024155086)
XLA Ops:
  1.3 29.6 %shard_map.113 = (f32[320,128]{1,0:T(8,128)S(1)}, f32[320,128]{1,0:T(8,128)S(1)}) custom-call(f32[320,128]{1,0:T(8,128)} %bitcast.11, f32[4,128]{1,0:T(4,128)} %absorption.1, f32[3,128]{1,0:T(4,128)} %geometry.1, f32[4,128]{1,0:T(4,128)} %penalty.1, s32[4,128]{1,0:T(4,128)} %link.1, s32[4,128]{1,0:T(4,128)} %orient.1, s32[1,8,32]{2,1,0:T(8,128)} %send_index.1, ...), custom_call_target="tpu_custom_call" | custom-call | flops 2000000000 | bytes 1000000 | tf_op jit(solution)/shard_map/pallas_call | solution.py:630
  30.9 0.7 %copy.15 = f32[4,4,20,128]{3,1,2,0:T(4,128)} copy(f32[4,4,20,128]{3,1,2,0:T(4,128)S(1)} %bitcast.10) | data formatting | bytes 327680
  31.6 0.7 %copy.16 = f32[4,4,20,128]{3,1,2,0:T(4,128)} copy(f32[4,4,20,128]{3,1,2,0:T(4,128)S(1)} %bitcast.9) | data formatting | bytes 327680

commit v4 on v3

--- a/solution.py
+++ b/solution.py
@@ -50,8 +50,8 @@
 
 
 ORDER = (3, 7, 2, 6, 1, 5, 0, 4)
-CUBE = 4
-DOWN = {0: (12, 1, 2, 3), 4: (8, 5, 6, 7)}
+NEAR, FAR = 0, 4
+DOWN = {NEAR: (1, 2, 12, 3, 13, 14, 15), FAR: (8, 11, 10, 9, 5, 6, 7)}
 EARLY = 4
 
 
@@ -133,8 +133,12 @@
     live_count,
     mass,
     stiffness,
-    solution_out,
-    residual_out,
+    direction_out,
+    second_out,
+    rhs_out,
+    applied_out,
+    twice_out,
+    weights_out,
     source_v,
     absorption_v,
     geometry_v,
@@ -190,27 +194,15 @@
     origins = [me - OFFSETS[q] for q in ORDER]
     along_x = [device(lax.rem(at_x + k, size_x), at_y, at_z, core) for k in range(1, size_x)]
     along_y = [device(at_x, lax.rem(at_y + k, size_y), at_z, core) for k in range(1, size_y)]
-    planes = [z for z in DOWN if z < size_z]
-    is_head = functools.reduce(jnp.logical_or, [at_z == z for z in planes])
-    is_relay = jnp.logical_and(lax.rem(at_z, CUBE) == 0, jnp.logical_not(is_head))
+    is_near = at_z == NEAR
+    is_far = at_z == FAR
+    has_far = FAR < size_z
     is_early = at_z < EARLY
 
     barrier = pltpu.get_barrier_semaphore()
 
     def greet(target):
         pl.semaphore_signal(barrier, inc=1, device_id=(target,), device_id_type=MESH)
-
-    for target in targets:
-        pl.when(inside(target))(functools.partial(greet, target))
-
-    @pl.when(is_head)
-    def _():
-        greet(device(at_x, at_y, at_z, 1 - core))
-        for target in along_x + along_y:
-            greet(target)
-        for k in range(1, size_z):
-            for c in range(2):
-                greet(device(at_x, at_y, lax.rem(at_z + k, size_z), c))
 
     loads = []
     for i, (src, dst) in enumerate(
@@ -227,9 +219,39 @@
             (stiffness, stiffness_v),
         )
     ):
-        copy = pltpu.make_async_copy(src, dst, in_sem.at[i])
+        loads.append(pltpu.make_async_copy(src, dst, in_sem.at[i]))
+    for copy in loads[:3]:
         copy.start()
-        loads.append(copy)
+    for target in targets:
+        pl.when(inside(target))(functools.partial(greet, target))
+
+    def greet_all(sources, place):
+        def one(k, carry):
+            target = place(k)
+            pl.when(target != me)(functools.partial(greet, target))
+            return carry
+
+        lax.fori_loop(0, sources, one, 0)
+
+    for copy in loads[3:]:
+        copy.start()
+    column = 2 * size_z
+
+    @pl.when(is_near)
+    def _():
+        for target in along_y:
+            greet(target)
+        greet_all(
+            size_x * column, lambda k: (k // column * size_y + at_y) * column + lax.rem(k, column)
+        )
+
+    if has_far:
+
+        @pl.when(is_far)
+        def _():
+            for target in along_x + along_y:
+                greet(target)
+            greet_all(column, lambda k: (at_x * size_y + at_y) * column + k)
 
     for copy in loads[:2]:
         copy.wait()
@@ -250,21 +272,21 @@
         )
 
     mine = at_z * 2 + core
-    up = [
-        remote(
-            own_best,
-            column_in.at[mine],
-            up_send.at[2 * i + c],
-            up_recv.at[mine],
-            device(at_x, at_y, z, c),
-        )
-        for i, z in enumerate(planes)
-        for c in range(2)
-    ]
-    up_to = [jnp.logical_not(jnp.logical_and(at_z == z, core == c)) for z in planes for c in range(2)]
+    slots = [((at_x * size_z + at_z) * 2 + core, NEAR, x) for x in range(size_x)]
+    if has_far:
+        slots.insert(1, (mine, FAR, at_x))
+    up, up_to = [], []
+    for slot, z, x in slots:
+        for c in range(2):
+            target = device(x, at_y, z, c)
+            up.append(
+                remote(own_best, column_in.at[slot], up_send.at[len(up)], up_recv.at[0], target)
+            )
+            up_to.append(target != me)
     partners = sum([inside(target).astype(jnp.int32) for target in targets])
     partners = partners + sum([wanted.astype(jnp.int32) for wanted in up_to])
-    partners = partners + is_head.astype(jnp.int32) * (len(along_x) + len(along_y))
+    partners = partners + is_near.astype(jnp.int32) * len(along_y)
+    partners = partners + is_far.astype(jnp.int32) * (len(along_x) + len(along_y))
 
     def send_up():
         pl.semaphore_wait(barrier, partners)
@@ -392,24 +414,24 @@
             for place in range(half * 4, half * 4 + 4):
                 pl.when(inside(targets[place]))(trades[trade][place].start)
 
-    def receive_traces(trade):
-        for place, copy in enumerate(trades[trade]):
-            pl.when(inside(origins[place]))(copy.wait_recv)
-        blocks = []
-        for j in range(4):
-            halves = []
-            for half in range(2):
+    def receive_traces(trade, near):
+        for half in range(2):
+            for place in range(half * 4, half * 4 + 4):
+                pl.when(inside(origins[place]))(trades[trade][place].wait_recv)
+            blocks = []
+            for j in range(4):
                 gathered = None
                 for g in range(4):
                     shift = (g - j) * SLOTS % LANES
                     part = incoming[trade, half * 4 + g]
                     part = pltpu.roll(part, shift, 1) if shift else part
                     gathered = part if gathered is None else jnp.where(group_of == g, part, gathered)
-                halves.append(gathered)
-            blocks.append(jnp.concatenate(halves, axis=1))
-        received = jnp.concatenate(blocks, axis=0)
-        high, low = split(received)
-        return jnp.concatenate([high, low], axis=0).astype(BF16)
+                blocks.append(gathered)
+            high, low = split(jnp.concatenate(blocks, axis=0))
+            received = jnp.concatenate([high, low], axis=0).astype(BF16)
+            both = dot(received, pick_remote[pl.ds(half * LANES, LANES), :])
+            near = near + (both[:ROWS] + both[ROWS:])
+        return near
 
     precondition(rhs[...], direction)
     fill_table(direction)
@@ -454,10 +476,9 @@
         flux_term = times(flux_weights[...], (value * geo_in[None]).reshape(FIELD, 2 * LANES))
         return both[:ROWS] + both[ROWS:], flux_term.reshape(NODES, 8, 2 * LANES)
 
-    def apply_remote(field, solved, local, received, target):
+    def apply_remote(trade, field, solved, local, target):
         near, flux_term = local
-        both = dot(received, pick_remote[...])
-        across = near + both[:ROWS] + both[ROWS:]
+        across = receive_traces(trade, near)
         total = [None] * NODES
         for t in range(TRI):
             sides = []
@@ -481,7 +502,7 @@
             value = value + pen_node[node] * field[node] - total[node]
             target[node] = live_two * value
 
-    across = [
+    across_x, across_y = [
         [
             remote(
                 level.at[step],
@@ -494,68 +515,84 @@
         ]
         for step, (first, line) in enumerate(((0, along_x), (len(along_x), along_y)))
     ]
-    down = {
-        z: [
-            remote(top, top, down_send.at[i], down_recv.at[0], device(at_x, at_y, to, core))
-            for i, to in enumerate(to for to in DOWN[z] if to < size_z)
+
+    def down(plane):
+        return [
+            remote(top, top, down_send.at[i], down_recv.at[0], device(at_x, at_y, z, core))
+            for i, z in enumerate(z for z in DOWN[plane] if z < size_z)
         ]
-        for z in planes
-    }
-    relays = [
-        remote(top, top, down_send.at[i], down_recv.at[0], device(at_x, at_y, at_z + i + 1, core))
-        for i in range(CUBE - 1)
-    ]
-
-    def column_slot(slot):
-        return remote(own_best, column_in.at[slot], up_send.at[0], up_recv.at[slot], me + 1 - 2 * core)
-
-    def meet_column():
-        column_in[mine] = own_best[...]
-        for k in range(1, size_z):
-            for c in range(2):
-                column_slot(lax.rem(at_z + k, size_z) * 2 + c).wait_recv()
-        column_slot(at_z * 2 + 1 - core).wait_recv()
-        level[0] = jnp.max(column_in[...], axis=0)
-        for copy in across[0]:
+
+    def meet_column(count, own, step, copies):
+        column_in[own] = own_best[...]
+        pltpu.make_async_copy(
+            column_in.at[pl.ds(0, count - 1)], column_in.at[pl.ds(0, count - 1)], up_recv.at[0]
+        ).wait()
+        level[step] = jnp.max(column_in[pl.ds(0, count)], axis=0)
+        for copy in copies:
             copy.start()
 
-    def meet_line(step, first):
+    def meet_line(step, first, copies):
         value = level[step]
-        for k, copy in enumerate(across[step]):
+        for k, copy in enumerate(copies):
             copy.wait_recv()
             value = jnp.maximum(value, along_in[first + k])
         return value
 
+    def meet_near():
+        meet_column(size_x * column, (at_x * size_z + at_z) * 2 + core, 1, across_y)
+
+    def meet_far():
+        meet_column(column, mine, 0, across_x)
+
     def meet_x():
-        level[1] = meet_line(0, 0)
-        for copy in across[1]:
+        level[1] = meet_line(0, 0, across_x)
+        for copy in across_y:
             copy.start()
 
-    def meet_y():
-        top[...] = meet_line(1, len(along_x))
-        for z in planes:
-
-            @pl.when(at_z == z)
-            def _(z=z):
-                for copy in down[z]:
-                    copy.start()
+    def meet_y(plane):
+        top[...] = meet_line(1, len(along_x), across_y)
+        for copy in down(plane):
+            copy.start()
+
+    def wait_all(copies):
+        for copy in copies:
+            copy.wait_send()
+
+    def write_out(field, target):
+        value = field[...]
+        for pair in range(2):
+            lanes = slice(pair * LANES, (pair + 1) * LANES)
+            for p in range(10):
+                even, odd = value[2 * p, :, lanes], value[2 * p + 1, :, lanes]
+                low, high = pair_up(even[None], odd[None])
+                target[pl.ds(160 * pair + 8 * p, 8), :] = low[0]
+                target[pl.ds(160 * pair + 80 + 8 * p, 8), :] = high[0]
 
     local = apply_local(direction)
-    pl.when(is_head)(meet_column)
-    apply_remote(direction, rhs, local, receive_traces(0), applied)
+    pl.when(is_near)(meet_near)
+    if has_far:
+        pl.when(is_far)(meet_far)
+    apply_remote(0, direction, rhs, local, applied)
     precondition(applied[...], second)
     fill_table(second)
     send_traces(1)
-    pl.when(is_head)(meet_x)
+    if has_far:
+        pl.when(is_far)(meet_x)
     local = apply_local(second)
-    pl.when(is_head)(meet_y)
-    apply_remote(second, applied, local, receive_traces(1), twice)
-    pl.when(jnp.logical_not(is_head))(down[0][0].wait_recv)
-
-    @pl.when(is_relay)
-    def _():
-        for copy in relays:
-            copy.start()
+    for field, target in (
+        (direction, direction_out),
+        (second, second_out),
+        (rhs, rhs_out),
+        (applied, applied_out),
+    ):
+        write_out(field, target)
+    pl.when(is_near)(functools.partial(meet_y, NEAR))
+    if has_far:
+        pl.when(is_far)(functools.partial(meet_y, FAR))
+    apply_remote(1, second, applied, local, twice)
+    write_out(twice, twice_out)
+    is_head = jnp.logical_or(is_near, is_far)
+    pl.when(jnp.logical_not(is_head))(down(NEAR)[0].wait_recv)
 
     upper = jnp.max(top[...], axis=1, keepdims=True)
     lower = 0.1 * upper
@@ -568,39 +605,17 @@
     step = 2.0 * ratio_new / half_width
     first_weight = inv_centre + ratio_new * ratio_now * inv_centre + step
     second_weight = -step * inv_centre
-    sol = first_weight * direction[...] + second_weight * second[...]
-    res = rhs[...] - first_weight * applied[...] - second_weight * twice[...]
-    for value, target in ((sol, solution_out), (res, residual_out)):
-        for pair in range(2):
-            lanes = slice(pair * LANES, (pair + 1) * LANES)
-            for p in range(10):
-                even, odd = value[2 * p, :, lanes], value[2 * p + 1, :, lanes]
-                low, high = pair_up(even[None], odd[None])
-                target[pl.ds(160 * pair + 8 * p, 8), :] = low[0]
-                target[pl.ds(160 * pair + 80 + 8 * p, 8), :] = high[0]
+    weights_out[0:1, :] = jnp.broadcast_to(first_weight, (1, LANES))
+    weights_out[1:2, :] = jnp.broadcast_to(second_weight, (1, LANES))
 
     for copies in trades:
         for place, copy in enumerate(copies):
             pl.when(inside(targets[place]))(copy.wait_send)
     for wanted, copy in zip(up_to, up):
         pl.when(wanted)(copy.wait_send)
-
-    @pl.when(is_head)
-    def _():
-        for copy in across[0] + across[1]:
-            copy.wait_send()
-
-    for z in planes:
-
-        @pl.when(at_z == z)
-        def _(z=z):
-            for copy in down[z]:
-                copy.wait_send()
-
-    @pl.when(is_relay)
-    def _():
-        for copy in relays:
-            copy.wait_send()
+    pl.when(is_near)(functools.partial(wait_all, across_y + down(NEAR)))
+    if has_far:
+        pl.when(is_far)(functools.partial(wait_all, across_x + across_y + down(FAR)))
 
 
 def solution(mesh):
@@ -627,11 +642,12 @@
         vmem = pltpu.VMEM
         field = vmem((NODES, 8, 2 * LANES), F32)
         dma = pltpu.SemaphoreType.DMA
-        outs = pl.pallas_call(
+        first, second, rhs, applied, twice, weights = pl.pallas_call(
             functools.partial(kernel, n),
-            out_shape=[jax.ShapeDtypeStruct(flat.shape, F32)] * 2,
+            out_shape=[jax.ShapeDtypeStruct(flat.shape, F32)] * 5
+            + [jax.ShapeDtypeStruct((2, LANES), F32)],
             in_specs=[pl.BlockSpec(memory_space=pltpu.HBM)] * 10,
-            out_specs=[pl.BlockSpec(memory_space=vmem)] * 2,
+            out_specs=[pl.BlockSpec(memory_space=vmem)] * 6,
             scratch_shapes=[
                 vmem((320, LANES), F32),
                 vmem((4, LANES), F32),
@@ -657,18 +673,18 @@
                 vmem((2, PEERS, PART, LANES), F32),
                 vmem((2, PEERS, PART, LANES), F32),
                 vmem((1, LANES), F32),
-                vmem((2 * size_z, 1, LANES), F32),
+                vmem((2 * size_z * size_x, 1, LANES), F32),
                 vmem((along, 1, LANES), F32),
                 vmem((2, 1, LANES), F32),
                 vmem((1, LANES), F32),
                 dma((10,)),
                 dma((2, PEERS)),
                 dma((2, PEERS)),
-                dma((2 * len(DOWN),)),
-                dma((2 * size_z,)),
+                dma((2 * size_x + 2,)),
+                dma((1,)),
                 dma((along,)),
                 dma((along,)),
-                dma((6,)),
+                dma((7,)),
                 dma((1,)),
             ],
             compiler_params=pltpu.CompilerParams(
@@ -681,6 +697,10 @@
                 value if value is live_count else pltpu.with_memory_space_constraint(value, pltpu.HBM)
                 for value in operands
             ]
+        )
+        outs = (
+            weights[0] * first + weights[1] * second,
+            rhs - weights[0] * applied - weights[1] * twice,
         )
         return tuple(
             out.reshape(GASES, NODES, COMPS, LANES).transpose(0, 2, 1, 3) for out in outs

time: 32.4 us -> 30.3 us (0.935)
  the two profiles are of different devices: /device:TPU:32 before, /device:TPU:1 now
where the time goes in v4:
time: 30.3 us; the launch traced here: 30 us
  Pallas kernels  28 us (92%)
  between operations  1.29 us (4%)
  other arithmetic  0.77 us (3%)
    pallas_call x1, Pallas kernels, body(): pl.pallas_call(functools.partial(kernel, n), out_shape=[jax.ShapeDtypeStr...  28 us
    sub x1, other arithmetic, body(): rhs - weights[0] * applied - weights[1] * twice  0.77 us

profile of v4, /device:TPU:1, one launch (start us, length us, event | category | flops | bytes accessed | tf_op | source)
XLA Modules:
  0.0 30.0 jit_solution(5499925362981557622)
XLA Ops:
  1.3 28.0 %shard_map.113 = (f32[320,128]{1,0:T(8,128)S(1)}, f32[320,128]{1,0:T(8,128)S(1)}, f32[320,128]{1,0:T(8,128)S(1)}, f32[320,128]{1,0:T(8,128)S(1)}, f32[320,128]{1,0:T(8,128)S(1)}, /*index=5*/f32[2,128]{1,0:T(2,128)S(1)}) custom-call(f32[320,128]{1,0:T(8,128)} %bitcast.15, f32[4,128]{1,0:T(4,128)} %absorption.1, f32[3,128]{1,0:T(4,128)} %geometry.1, ...), custom_call_target="tpu_custom_call" | custom-call | flops 2000000000 | bytes 1000000 | tf_op jit(solution)/shard_map/pallas_call | solution.py:645
  29.3 0.8 %multiply_subtract_fusion = (f32[320,128]{1,0:T(8,128)}, f32[320,128]{1,0:T(8,128)}) fusion(f32[320,128]{1,0:T(8,128)S(1)} %get-tuple-element.13, f32[320,128]{1,0:T(8,128)S(1)} %get-tuple-element.11, f32[320,128]{1,0:T(8,128)S(1)} %get-tuple-element.12, f32[128]{0:T(128)S(1)} %get-tuple-element.17, f32[128]{0:T(128)S(1)} %get-tuple-element.16, ...), kind=kLoop, calls=%fused_computation | loop fusion | flops 286720 | bytes 1147904 | tf_op jit(solution)/shard_map/sub | solution.py:703
  (1 shorter events, 0.0 us)

commit v5 on v4

--- a/solution.py
+++ b/solution.py
@@ -49,9 +49,22 @@
 FACE_NODE, TURNED = node_tables()
 
 
-ORDER = (3, 7, 2, 6, 1, 5, 0, 4)
-NEAR, FAR = 0, 4
-DOWN = {NEAR: (1, 2, 12, 3, 13, 14, 15), FAR: (8, 11, 10, 9, 5, 6, 7)}
+def step_weights():
+    centre, half_width = (1.0 + 0.1) / 2.0, (1.0 - 0.1) / 2.0
+    sigma_one = centre / half_width
+    ratio = 1.0 / sigma_one
+    ratio_new = 1.0 / (2.0 * sigma_one - ratio)
+    step = 2.0 * ratio_new / half_width
+    return (1.0 + ratio_new * ratio) / centre + step, -step / centre
+
+
+FIRST_WEIGHT, SECOND_WEIGHT = step_weights()
+
+
+ORDER = (7, 6, 5, 4, 3, 2, 1, 0)
+DOWN = (4, 1, 5, 2, 3, 8, 12, 9, 10, 11)
+RELAY = {4: (6, 7), 12: (13, 14, 15)}
+REACH = 4
 EARLY = 4
 
 
@@ -126,7 +139,7 @@
     source,
     absorption,
     geometry,
-    penalty,
+    penalty_v,
     link,
     orient,
     send_index,
@@ -142,11 +155,9 @@
     source_v,
     absorption_v,
     geometry_v,
-    penalty_v,
     link_v,
     orient_v,
     send_v,
-    live_v,
     mass_v,
     stiffness_v,
     rhs,
@@ -162,6 +173,7 @@
     table,
     outgoing,
     incoming,
+    held,
     own_best,
     column_in,
     along_in,
@@ -170,6 +182,8 @@
     in_sem,
     send_sem,
     recv_sem,
+    held_send,
+    held_recv,
     up_send,
     up_recv,
     along_send,
@@ -194,10 +208,23 @@
     origins = [me - OFFSETS[q] for q in ORDER]
     along_x = [device(lax.rem(at_x + k, size_x), at_y, at_z, core) for k in range(1, size_x)]
     along_y = [device(at_x, lax.rem(at_y + k, size_y), at_z, core) for k in range(1, size_y)]
-    is_near = at_z == NEAR
-    is_far = at_z == FAR
-    has_far = FAR < size_z
+    is_head = at_z == 0
     is_early = at_z < EARLY
+
+    column = 2 * size_z
+    plane = column * size_y
+    across_planes = size_x > 1 and size_z >= 4
+    in_plane = lax.rem(me, plane)
+    passed = in_plane - (plane - column)
+    is_passing = jnp.logical_and(
+        jnp.logical_and(passed >= 0, passed < REACH), jnp.logical_and(me + column < n, across_planes)
+    )
+    is_detoured = jnp.logical_and(
+        in_plane < REACH, jnp.logical_and(me >= plane, across_planes)
+    )
+
+    def detours(reach):
+        return jnp.logical_and(is_detoured, in_plane < reach)
 
     barrier = pltpu.get_barrier_semaphore()
 
@@ -207,8 +234,6 @@
     loads = []
     for i, (src, dst) in enumerate(
         (
-            (penalty, penalty_v),
-            (live_count, live_v),
             (mass, mass_v),
             (send_index, send_v),
             (source, source_v),
@@ -220,42 +245,30 @@
         )
     ):
         loads.append(pltpu.make_async_copy(src, dst, in_sem.at[i]))
-    for copy in loads[:3]:
+    loads[0].start()
+    for reach in range(REACH, 0, -1):
+        pl.when(inside(me - reach))(functools.partial(greet, me - reach))
+        ahead = me + reach
+        over = jnp.logical_and(in_plane + reach >= plane, across_planes)
+        pl.when(inside(ahead))(functools.partial(greet, jnp.where(over, ahead - column, ahead)))
+    pl.when(is_passing)(functools.partial(greet, me + column))
+
+    for copy in loads[1:]:
         copy.start()
-    for target in targets:
-        pl.when(inside(target))(functools.partial(greet, target))
-
-    def greet_all(sources, place):
-        def one(k, carry):
-            target = place(k)
-            pl.when(target != me)(functools.partial(greet, target))
-            return carry
-
-        lax.fori_loop(0, sources, one, 0)
-
-    for copy in loads[3:]:
-        copy.start()
-    column = 2 * size_z
-
-    @pl.when(is_near)
+    @pl.when(is_head)
     def _():
+        for z in sorted(range(1, size_z), key=lambda z: abs(z - size_z // 2 - 1)):
+            for x in range(size_x):
+                for c in range(2):
+                    greet(device(x, at_y, z, c))
+        greet(device(at_x, at_y, at_z, 1 - core))
+        for target in along_x:
+            for c in range(2):
+                greet(target - core + c)
         for target in along_y:
             greet(target)
-        greet_all(
-            size_x * column, lambda k: (k // column * size_y + at_y) * column + lax.rem(k, column)
-        )
-
-    if has_far:
-
-        @pl.when(is_far)
-        def _():
-            for target in along_x + along_y:
-                greet(target)
-            greet_all(column, lambda k: (at_x * size_y + at_y) * column + k)
-
-    for copy in loads[:2]:
-        copy.wait()
-    live = (iota((1, LANES), 1) < live_v[0]).astype(F32)
+
+    live = (iota((1, LANES), 1) < live_count[0]).astype(F32)
     pen = [penalty_v[f : f + 1, :] for f in range(FACES)]
     pen_sum = pen[0] + pen[1] + pen[2] + pen[3]
     best = jnp.where(live > 0.5, 1.0 + 0.25 * pen_sum, 0.0)
@@ -271,31 +284,43 @@
             device_id_type=MESH,
         )
 
-    mine = at_z * 2 + core
-    slots = [((at_x * size_z + at_z) * 2 + core, NEAR, x) for x in range(size_x)]
-    if has_far:
-        slots.insert(1, (mine, FAR, at_x))
+    mine = at_x * column + at_z * 2 + core
     up, up_to = [], []
-    for slot, z, x in slots:
+    for x in range(size_x):
         for c in range(2):
-            target = device(x, at_y, z, c)
+            target = device(x, at_y, 0, c)
             up.append(
-                remote(own_best, column_in.at[slot], up_send.at[len(up)], up_recv.at[0], target)
+                remote(own_best, column_in.at[mine], up_send.at[len(up)], up_recv.at[0], target)
             )
             up_to.append(target != me)
-    partners = sum([inside(target).astype(jnp.int32) for target in targets])
-    partners = partners + sum([wanted.astype(jnp.int32) for wanted in up_to])
-    partners = partners + is_near.astype(jnp.int32) * len(along_y)
-    partners = partners + is_far.astype(jnp.int32) * (len(along_x) + len(along_y))
+
+    def count(wanted):
+        return sum([each.astype(jnp.int32) for each in wanted])
+
+    partners = count(up_to) + is_head.astype(jnp.int32) * len(along_y)
+    partners = partners + count([inside(me + reach) for reach in range(1, REACH + 1)])
+    partners = partners + count(
+        [
+            jnp.logical_and(inside(me - reach), jnp.logical_not(detours(reach)))
+            for reach in range(1, REACH + 1)
+        ]
+    )
+    partners = partners + is_detoured.astype(jnp.int32)
+    partners = partners + is_passing.astype(jnp.int32) * (REACH - passed)
+
+    def await_partners():
+        pl.semaphore_wait(barrier, partners)
 
     def send_up():
-        pl.semaphore_wait(barrier, partners)
         for wanted, copy in zip(up_to, up):
             pl.when(wanted)(copy.start)
 
-    pl.when(jnp.logical_not(is_early))(send_up)
-
-    for copy in loads[2:]:
+    @pl.when(jnp.logical_not(is_early))
+    def _():
+        await_partners()
+        send_up()
+
+    for copy in loads:
         copy.wait()
 
     rows = spread_rows()
@@ -385,22 +410,50 @@
 
     group_of = iota((PART, LANES), 1) // SLOTS
 
-    def trade_copies(trade):
-        return [
-            remote(
-                outgoing.at[trade, place],
-                incoming.at[trade, place],
-                send_sem.at[trade, place],
-                recv_sem.at[trade, place],
-                targets[place],
-            )
-            for place in range(PEERS)
-        ]
-
-    trades = [trade_copies(0), trade_copies(1)]
+    nearer = (at_z >= size_z // 2).astype(jnp.int32)
+
+    def peer(half, g):
+        reach = PEERS // 2 - g
+        return jnp.where(half == 0, me - reach, me + reach), jnp.where(half == 0, me + reach, me - reach)
+
+    def trade_copy(trade, half, g):
+        place = half * 4 + g
+        return remote(
+            outgoing.at[trade, place],
+            incoming.at[trade, place],
+            send_sem.at[trade, place],
+            recv_sem.at[trade, place],
+            peer(half, g)[0],
+        )
+
+    def detour_copy(g):
+        return remote(
+            outgoing.at[0, g], held.at[g], send_sem.at[0, g], held_recv.at[g], me - column
+        )
+
+    def pass_copy(g):
+        return remote(
+            held.at[g],
+            incoming.at[0, g],
+            held_send.at[g],
+            recv_sem.at[0, g],
+            me + column - (REACH - g),
+        )
+
+    def pass_on():
+        for g in range(REACH):
+
+            @pl.when(passed < REACH - g)
+            def _(g=g):
+                detour_copy(g).wait_recv()
+                pass_copy(g).start()
+
+    def pass_done():
+        for g in range(REACH):
+            pl.when(passed < REACH - g)(pass_copy(g).wait_send)
 
     def send_traces(trade):
-        for half in range(2):
+        for at, half in enumerate((nearer, 1 - nearer)):
             both = dot(table[...], pick_send[half])
             packed = both[:ROWS] + both[ROWS:]
             parts = [packed[j * PART : (j + 1) * PART] for j in range(4)]
@@ -411,13 +464,21 @@
                     part = pltpu.roll(parts[j], shift, 1) if shift else parts[j]
                     message = part if message is None else jnp.where(group_of == j, part, message)
                 outgoing[trade, half * 4 + g] = message
-            for place in range(half * 4, half * 4 + 4):
-                pl.when(inside(targets[place]))(trades[trade][place].start)
+            if trade == 0 and at == 0:
+                pl.when(is_early)(await_partners)
+                pl.when(is_passing)(pass_on)
+            for g in range(4):
+                wanted = inside(peer(half, g)[0])
+                if trade == 0:
+                    detour = jnp.logical_and(half == 0, detours(REACH - g))
+                    pl.when(detour)(detour_copy(g).start)
+                    wanted = jnp.logical_and(wanted, jnp.logical_not(detour))
+                pl.when(wanted)(trade_copy(trade, half, g).start)
 
     def receive_traces(trade, near):
-        for half in range(2):
-            for place in range(half * 4, half * 4 + 4):
-                pl.when(inside(origins[place]))(trades[trade][place].wait_recv)
+        for half in (nearer, 1 - nearer):
+            for g in range(4):
+                pl.when(inside(peer(half, g)[1]))(trade_copy(trade, half, g).wait_recv)
             blocks = []
             for j in range(4):
                 gathered = None
@@ -429,14 +490,14 @@
                 blocks.append(gathered)
             high, low = split(jnp.concatenate(blocks, axis=0))
             received = jnp.concatenate([high, low], axis=0).astype(BF16)
-            both = dot(received, pick_remote[pl.ds(half * LANES, LANES), :])
+            both = dot(received, pick_remote[pl.ds(pl.multiple_of(half * LANES, LANES), LANES), :])
             near = near + (both[:ROWS] + both[ROWS:])
         return near
 
     precondition(rhs[...], direction)
     fill_table(direction)
+    send_traces(0)
     pl.when(is_early)(send_up)
-    send_traces(0)
 
     flux = jnp.zeros(square, F32)
     for d in range(3):
@@ -502,56 +563,35 @@
             value = value + pen_node[node] * field[node] - total[node]
             target[node] = live_two * value
 
-    across_x, across_y = [
-        [
-            remote(
-                level.at[step],
-                along_in.at[first + k],
-                along_send.at[first + k],
-                along_recv.at[first + k],
-                target,
-            )
-            for k, target in enumerate(line)
-        ]
-        for step, (first, line) in enumerate(((0, along_x), (len(along_x), along_y)))
+    across = [
+        remote(level, along_in.at[k], along_send.at[k], along_recv.at[k], target)
+        for k, target in enumerate(along_y)
     ]
 
-    def down(plane):
+    def down(chips):
         return [
             remote(top, top, down_send.at[i], down_recv.at[0], device(at_x, at_y, z, core))
-            for i, z in enumerate(z for z in DOWN[plane] if z < size_z)
+            for i, z in enumerate(z for z in chips if z < size_z)
         ]
 
-    def meet_column(count, own, step, copies):
-        column_in[own] = own_best[...]
-        pltpu.make_async_copy(
-            column_in.at[pl.ds(0, count - 1)], column_in.at[pl.ds(0, count - 1)], up_recv.at[0]
-        ).wait()
-        level[step] = jnp.max(column_in[pl.ds(0, count)], axis=0)
+    def meet_column():
+        column_in[mine] = own_best[...]
+        rest = column_in.at[pl.ds(0, size_x * column - 1)]
+        pltpu.make_async_copy(rest, rest, up_recv.at[0]).wait()
+        level[...] = jnp.max(column_in[...], axis=0)
+        for copy in across:
+            copy.start()
+
+    def meet_line():
+        value = level[...]
+        for k, copy in enumerate(across):
+            copy.wait_recv()
+            value = jnp.maximum(value, along_in[k])
+        top[...] = value
+        start_all(down(DOWN))
+
+    def start_all(copies):
         for copy in copies:
-            copy.start()
-
-    def meet_line(step, first, copies):
-        value = level[step]
-        for k, copy in enumerate(copies):
-            copy.wait_recv()
-            value = jnp.maximum(value, along_in[first + k])
-        return value
-
-    def meet_near():
-        meet_column(size_x * column, (at_x * size_z + at_z) * 2 + core, 1, across_y)
-
-    def meet_far():
-        meet_column(column, mine, 0, across_x)
-
-    def meet_x():
-        level[1] = meet_line(0, 0, across_x)
-        for copy in across_y:
-            copy.start()
-
-    def meet_y(plane):
-        top[...] = meet_line(1, len(along_x), across_y)
-        for copy in down(plane):
             copy.start()
 
     def wait_all(copies):
@@ -569,15 +609,11 @@
                 target[pl.ds(160 * pair + 80 + 8 * p, 8), :] = high[0]
 
     local = apply_local(direction)
-    pl.when(is_near)(meet_near)
-    if has_far:
-        pl.when(is_far)(meet_far)
+    pl.when(is_head)(meet_column)
     apply_remote(0, direction, rhs, local, applied)
     precondition(applied[...], second)
     fill_table(second)
     send_traces(1)
-    if has_far:
-        pl.when(is_far)(meet_x)
     local = apply_local(second)
     for field, target in (
         (direction, direction_out),
@@ -586,42 +622,35 @@
         (applied, applied_out),
     ):
         write_out(field, target)
-    pl.when(is_near)(functools.partial(meet_y, NEAR))
-    if has_far:
-        pl.when(is_far)(functools.partial(meet_y, FAR))
+    pl.when(is_head)(meet_line)
     apply_remote(1, second, applied, local, twice)
     write_out(twice, twice_out)
-    is_head = jnp.logical_or(is_near, is_far)
-    pl.when(jnp.logical_not(is_head))(down(NEAR)[0].wait_recv)
-
-    upper = jnp.max(top[...], axis=1, keepdims=True)
-    lower = 0.1 * upper
-    centre = (upper + lower) / 2.0
-    half_width = (upper - lower) / 2.0
-    sigma_one = centre / half_width
-    ratio_now = 1.0 / sigma_one
-    ratio_new = 1.0 / (2.0 * sigma_one - ratio_now)
-    inv_centre = 1.0 / centre
-    step = 2.0 * ratio_new / half_width
-    first_weight = inv_centre + ratio_new * ratio_now * inv_centre + step
-    second_weight = -step * inv_centre
+    for trade in range(2):
+        for place, target in enumerate(targets):
+            half, g = divmod(place, 4)
+            pl.when(inside(target))(trade_copy(trade, half, g).wait_send)
+    for wanted, copy in zip(up_to, up):
+        pl.when(wanted)(copy.wait_send)
+    pl.when(is_passing)(pass_done)
+    pl.when(jnp.logical_not(is_head))(down(DOWN)[0].wait_recv)
+    for z, chips in RELAY.items():
+        pl.when(at_z == z)(functools.partial(start_all, down(chips)))
+
+    inv_upper = 1.0 / jnp.max(top[...], axis=1, keepdims=True)
+    first_weight = FIRST_WEIGHT * inv_upper
+    second_weight = SECOND_WEIGHT * (inv_upper * inv_upper)
     weights_out[0:1, :] = jnp.broadcast_to(first_weight, (1, LANES))
     weights_out[1:2, :] = jnp.broadcast_to(second_weight, (1, LANES))
 
-    for copies in trades:
-        for place, copy in enumerate(copies):
-            pl.when(inside(targets[place]))(copy.wait_send)
-    for wanted, copy in zip(up_to, up):
-        pl.when(wanted)(copy.wait_send)
-    pl.when(is_near)(functools.partial(wait_all, across_y + down(NEAR)))
-    if has_far:
-        pl.when(is_far)(functools.partial(wait_all, across_x + across_y + down(FAR)))
+    pl.when(is_head)(functools.partial(wait_all, across + down(DOWN)))
+    for z, chips in RELAY.items():
+        pl.when(at_z == z)(functools.partial(wait_all, down(chips)))
 
 
 def solution(mesh):
     n = mesh.shape["dom"]
     size_x, size_y, size_z = torus(n)
-    along = max(size_x + size_y - 2, 1)
+    along = max(size_y - 1, 1)
 
     def body(
         source, absorption, geometry, penalty, link, orient, send_index, live_count, mass, stiffness
@@ -642,21 +671,24 @@
         vmem = pltpu.VMEM
         field = vmem((NODES, 8, 2 * LANES), F32)
         dma = pltpu.SemaphoreType.DMA
+        hbm = pl.BlockSpec(memory_space=pltpu.HBM)
         first, second, rhs, applied, twice, weights = pl.pallas_call(
             functools.partial(kernel, n),
             out_shape=[jax.ShapeDtypeStruct(flat.shape, F32)] * 5
             + [jax.ShapeDtypeStruct((2, LANES), F32)],
-            in_specs=[pl.BlockSpec(memory_space=pltpu.HBM)] * 10,
+            in_specs=[hbm] * 3
+            + [pl.BlockSpec(memory_space=vmem)]
+            + [hbm] * 3
+            + [pl.BlockSpec(memory_space=pltpu.SMEM)]
+            + [hbm] * 2,
             out_specs=[pl.BlockSpec(memory_space=vmem)] * 6,
             scratch_shapes=[
                 vmem((320, LANES), F32),
                 vmem((4, LANES), F32),
                 vmem((3, LANES), F32),
-                vmem((4, LANES), F32),
                 vmem((4, LANES), jnp.int32),
                 vmem((4, LANES), jnp.int32),
                 vmem((1, PEERS, SLOTS), jnp.int32),
-                pltpu.SMEM((1,), jnp.int32),
                 vmem((NODES, NODES), F32),
                 vmem((3, NODES, NODES), F32),
                 field,
@@ -672,19 +704,22 @@
                 vmem((2 * ROWS, LOCAL), BF16),
                 vmem((2, PEERS, PART, LANES), F32),
                 vmem((2, PEERS, PART, LANES), F32),
+                vmem((REACH, PART, LANES), F32),
                 vmem((1, LANES), F32),
                 vmem((2 * size_z * size_x, 1, LANES), F32),
                 vmem((along, 1, LANES), F32),
-                vmem((2, 1, LANES), F32),
                 vmem((1, LANES), F32),
-                dma((10,)),
+                vmem((1, LANES), F32),
+                dma((8,)),
                 dma((2, PEERS)),
                 dma((2, PEERS)),
-                dma((2 * size_x + 2,)),
+                dma((REACH,)),
+                dma((REACH,)),
+                dma((2 * size_x,)),
                 dma((1,)),
                 dma((along,)),
                 dma((along,)),
-                dma((7,)),
+                dma((len(DOWN),)),
                 dma((1,)),
             ],
             compiler_params=pltpu.CompilerParams(
@@ -694,7 +729,9 @@
                 flops=2_000_000_000, bytes_accessed=1_000_000, transcendentals=0
             ),
         )(*[
-                value if value is live_count else pltpu.with_memory_space_constraint(value, pltpu.HBM)
+                value
+                if value is live_count or value is penalty
+                else pltpu.with_memory_space_constraint(value, pltpu.HBM)
                 for value in operands
             ]
         )

time: 30.3 us -> 29.6 us (0.977)
  the two profiles are of different devices: /device:TPU:1 before, /device:TPU:32 now
where the time goes in v5:
time: 29.6 us; the launch traced here: 29.4 us
  Pallas kernels  27.3 us (92%)
  between operations  1.32 us (4%)
  other arithmetic  0.77 us (3%)
    pallas_call x1, Pallas kernels, body(): pl.pallas_call(functools.partial(kernel, n), out_shape=[jax.ShapeDtypeStr...  27.3 us
    sub x1, other arithmetic, body(): rhs - weights[0] * applied - weights[1] * twice  0.77 us

profile of v5, /device:TPU:32, one launch (start us, length us, event | category | flops | bytes accessed | tf_op | source)
XLA Modules:
  0.0 29.4 jit_solution(3853343362784353796)
XLA Ops:
  0.6 0.0 copy-start
  1.3 0.0 copy-done
  1.3 27.3 %shard_map.113 = (f32[320,128]{1,0:T(8,128)S(1)}, f32[320,128]{1,0:T(8,128)S(1)}, f32[320,128]{1,0:T(8,128)S(1)}, f32[320,128]{1,0:T(8,128)S(1)}, f32[320,128]{1,0:T(8,128)S(1)}, /*index=5*/f32[2,128]{1,0:T(2,128)S(1)}) custom-call(f32[320,128]{1,0:T(8,128)} %bitcast.15, f32[4,128]{1,0:T(4,128)} %absorption.1, f32[3,128]{1,0:T(4,128)} %geometry.1, ...), custom_call_target="tpu_custom_call" | custom-call | flops 2000000000 | bytes 1000000 | tf_op jit(solution)/shard_map/pallas_call | solution.py:675
  28.6 0.8 %multiply_subtract_fusion = (f32[320,128]{1,0:T(8,128)}, f32[320,128]{1,0:T(8,128)}) fusion(f32[320,128]{1,0:T(8,128)S(1)} %get-tuple-element.13, f32[320,128]{1,0:T(8,128)S(1)} %get-tuple-element.11, f32[320,128]{1,0:T(8,128)S(1)} %get-tuple-element.12, f32[128]{0:T(128)S(1)} %get-tuple-element.17, f32[128]{0:T(128)S(1)} %get-tuple-element.16, ...), kind=kLoop, calls=%fused_computation | loop fusion | flops 286720 | bytes 1147904 | tf_op jit(solution)/shard_map/sub | solution.py:740
  (1 shorter events, 0.0 us)
Async XLA Ops:
  0.6 0.7 %copy-start = (f32[4,128]{1,0:T(4,128)S(1)}, f32[4,128]{1,0:T(4,128)}, u32[]{:S(2)}) copy-start(f32[4,128]{1,0:T(4,128)} %penalty_v.1) | copy-start | bytes 6148

commit v6 on v5

--- a/solution.py
+++ b/solution.py
@@ -64,6 +64,7 @@
 ORDER = (7, 6, 5, 4, 3, 2, 1, 0)
 DOWN = (4, 1, 5, 2, 3, 8, 12, 9, 10, 11)
 RELAY = {4: (6, 7), 12: (13, 14, 15)}
+LOOKOUT = (4, 1, 2)
 REACH = 4
 EARLY = 4
 
@@ -177,6 +178,7 @@
     own_best,
     column_in,
     along_in,
+    look_in,
     level,
     top,
     in_sem,
@@ -188,6 +190,8 @@
     up_recv,
     along_send,
     along_recv,
+    look_send,
+    look_recv,
     down_send,
     down_recv,
 ):
@@ -206,9 +210,14 @@
 
     targets = [me + OFFSETS[q] for q in ORDER]
     origins = [me - OFFSETS[q] for q in ORDER]
+    other_y = [k + (k >= at_y).astype(jnp.int32) for k in range(size_y - 1)]
     along_x = [device(lax.rem(at_x + k, size_x), at_y, at_z, core) for k in range(1, size_x)]
-    along_y = [device(at_x, lax.rem(at_y + k, size_y), at_z, core) for k in range(1, size_y)]
+    along_y = [device(at_x, y, at_z, core) for y in other_y]
+    lookouts = [z for z in LOOKOUT if z < size_z]
     is_head = at_z == 0
+    is_lookout = jnp.logical_and(
+        at_y == 0, functools.reduce(jnp.logical_or, [at_z == z for z in lookouts])
+    )
     is_early = at_z < EARLY
 
     column = 2 * size_z
@@ -255,6 +264,11 @@
 
     for copy in loads[1:]:
         copy.start()
+    @pl.when(is_lookout)
+    def _():
+        for y in range(1, size_y):
+            greet(device(at_x, y, 0, core))
+
     @pl.when(is_head)
     def _():
         for z in sorted(range(1, size_z), key=lambda z: abs(z - size_z // 2 - 1)):
@@ -306,6 +320,7 @@
         ]
     )
     partners = partners + is_detoured.astype(jnp.int32)
+    partners = partners + jnp.logical_and(is_head, at_y > 0).astype(jnp.int32) * len(lookouts)
     partners = partners + is_passing.astype(jnp.int32) * (REACH - passed)
 
     def await_partners():
@@ -563,10 +578,26 @@
             value = value + pen_node[node] * field[node] - total[node]
             target[node] = live_two * value
 
-    across = [
-        remote(level, along_in.at[k], along_send.at[k], along_recv.at[k], target)
-        for k, target in enumerate(along_y)
+    across = []
+    for k, y in enumerate(other_y):
+        slot = at_y - (at_y > y).astype(jnp.int32)
+        target = device(at_x, y, at_z, core)
+        across.append(
+            remote(level, along_in.at[slot], along_send.at[k], along_recv.at[slot], target)
+        )
+    ahead_of = [
+        remote(
+            level, look_in.at[at_y], look_send.at[i], look_recv.at[at_y], device(at_x, 0, z, core)
+        )
+        for i, z in enumerate(lookouts)
     ]
+
+    def look_out():
+        value = None
+        for y in range(size_y):
+            remote(level, look_in.at[y], look_send.at[0], look_recv.at[y], me + 1 - 2 * core).wait_recv()
+            value = look_in[y] if value is None else jnp.maximum(value, look_in[y])
+        top[...] = value
 
     def down(chips):
         return [
@@ -574,21 +605,36 @@
             for i, z in enumerate(z for z in chips if z < size_z)
         ]
 
+    down_to = [
+        jnp.logical_or(at_y > 0, z not in lookouts) for z in DOWN if z < size_z
+    ]
+
+    def heads_done():
+        wait_all(across + ahead_of)
+        for wanted, copy in zip(down_to, down(DOWN)):
+            pl.when(wanted)(copy.wait_send)
+
     def meet_column():
         column_in[mine] = own_best[...]
         rest = column_in.at[pl.ds(0, size_x * column - 1)]
         pltpu.make_async_copy(rest, rest, up_recv.at[0]).wait()
-        level[...] = jnp.max(column_in[...], axis=0)
-        for copy in across:
-            copy.start()
+        chains = column_in[...].reshape(8, size_x * column // 8, 1, LANES)
+        level[...] = jnp.max(jnp.max(chains, axis=0), axis=0)
+        if across:
+            pl.when(at_y > 0)(across[0].start)
+        start_all(ahead_of)
+        if across:
+            pl.when(at_y == 0)(across[0].start)
+        start_all(across[1:])
 
     def meet_line():
         value = level[...]
-        for k, copy in enumerate(across):
-            copy.wait_recv()
+        for k in range(size_y - 1):
+            remote(level, along_in.at[k], along_send.at[k], along_recv.at[k], me + 1 - 2 * core).wait_recv()
             value = jnp.maximum(value, along_in[k])
         top[...] = value
-        start_all(down(DOWN))
+        for wanted, copy in zip(down_to, down(DOWN)):
+            pl.when(wanted)(copy.start)
 
     def start_all(copies):
         for copy in copies:
@@ -632,7 +678,8 @@
     for wanted, copy in zip(up_to, up):
         pl.when(wanted)(copy.wait_send)
     pl.when(is_passing)(pass_done)
-    pl.when(jnp.logical_not(is_head))(down(DOWN)[0].wait_recv)
+    pl.when(is_lookout)(look_out)
+    pl.when(jnp.logical_not(jnp.logical_or(is_head, is_lookout)))(down(DOWN)[0].wait_recv)
     for z, chips in RELAY.items():
         pl.when(at_z == z)(functools.partial(start_all, down(chips)))
 
@@ -642,7 +689,7 @@
     weights_out[0:1, :] = jnp.broadcast_to(first_weight, (1, LANES))
     weights_out[1:2, :] = jnp.broadcast_to(second_weight, (1, LANES))
 
-    pl.when(is_head)(functools.partial(wait_all, across + down(DOWN)))
+    pl.when(is_head)(heads_done)
     for z, chips in RELAY.items():
         pl.when(at_z == z)(functools.partial(wait_all, down(chips)))
 
@@ -708,6 +755,7 @@
                 vmem((1, LANES), F32),
                 vmem((2 * size_z * size_x, 1, LANES), F32),
                 vmem((along, 1, LANES), F32),
+                vmem((size_y, 1, LANES), F32),
                 vmem((1, LANES), F32),
                 vmem((1, LANES), F32),
                 dma((8,)),
@@ -719,6 +767,8 @@
                 dma((1,)),
                 dma((along,)),
                 dma((along,)),
+                dma((len(LOOKOUT),)),
+                dma((size_y,)),
                 dma((len(DOWN),)),
                 dma((1,)),
             ],

time: 29.6 us -> 28.7 us (0.970)
  the two profiles are of different devices: /device:TPU:32 before, /device:TPU:1 now
where the time goes in v6:
time: 28.7 us; the launch traced here: 28.4 us
  Pallas kernels  26.3 us (92%)
  between operations  1.32 us (5%)
  other arithmetic  0.77 us (3%)
    pallas_call x1, Pallas kernels, body(): pl.pallas_call(functools.partial(kernel, n), out_shape=[jax.ShapeDtypeStr...  26.3 us
    sub x1, other arithmetic, body(): rhs - weights[0] * applied - weights[1] * twice  0.77 us

profile of v6, /device:TPU:1, one launch (start us, length us, event | category | flops | bytes accessed | tf_op | source)
XLA Modules:
  0.0 28.4 jit_solution(9577480197630515508)
XLA Ops:
  0.6 0.0 copy-start
  1.3 0.0 copy-done
  1.3 26.3 %shard_map.113 = (f32[320,128]{1,0:T(8,128)S(1)}, f32[320,128]{1,0:T(8,128)S(1)}, f32[320,128]{1,0:T(8,128)S(1)}, f32[320,128]{1,0:T(8,128)S(1)}, f32[320,128]{1,0:T(8,128)S(1)}, /*index=5*/f32[2,128]{1,0:T(2,128)S(1)}) custom-call(f32[320,128]{1,0:T(8,128)} %bitcast.15, f32[4,128]{1,0:T(4,128)} %absorption.1, f32[3,128]{1,0:T(4,128)} %geometry.1, ...), custom_call_target="tpu_custom_call" | custom-call | flops 2000000000 | bytes 1000000 | tf_op jit(solution)/shard_map/pallas_call | solution.py:722
  27.6 0.8 %multiply_subtract_fusion = (f32[320,128]{1,0:T(8,128)}, f32[320,128]{1,0:T(8,128)}) fusion(f32[320,128]{1,0:T(8,128)S(1)} %get-tuple-element.13, f32[320,128]{1,0:T(8,128)S(1)} %get-tuple-element.11, f32[320,128]{1,0:T(8,128)S(1)} %get-tuple-element.12, f32[128]{0:T(128)S(1)} %get-tuple-element.17, f32[128]{0:T(128)S(1)} %get-tuple-element.16, ...), kind=kLoop, calls=%fused_computation | loop fusion | flops 286720 | bytes 1147904 | tf_op jit(solution)/shard_map/sub | solution.py:790
  (1 shorter events, 0.0 us)
Async XLA Ops:
  0.6 0.7 %copy-start = (f32[4,128]{1,0:T(4,128)S(1)}, f32[4,128]{1,0:T(4,128)}, u32[]{:S(2)}) copy-start(f32[4,128]{1,0:T(4,128)} %penalty_v.1) | copy-start | bytes 6148

commit v7 on v6

--- a/solution.py
+++ b/solution.py
@@ -62,7 +62,7 @@
 
 
 ORDER = (7, 6, 5, 4, 3, 2, 1, 0)
-DOWN = (4, 1, 5, 2, 3, 8, 12, 9, 10, 11)
+DOWN = (4, 1, 2, 3, 5, 8, 12, 9, 10, 11)
 RELAY = {4: (6, 7), 12: (13, 14, 15)}
 LOOKOUT = (4, 1, 2)
 REACH = 4
@@ -635,6 +635,7 @@
         top[...] = value
         for wanted, copy in zip(down_to, down(DOWN)):
             pl.when(wanted)(copy.start)
+        write_weights()
 
     def start_all(copies):
         for copy in copies:
@@ -643,6 +644,18 @@
     def wait_all(copies):
         for copy in copies:
             copy.wait_send()
+
+    def sends_done(trade):
+        for place, target in enumerate(targets):
+            half, g = divmod(place, 4)
+            pl.when(inside(target))(trade_copy(trade, half, g).wait_send)
+
+    def write_weights():
+        inv_upper = 1.0 / jnp.max(top[...], axis=1, keepdims=True)
+        first_weight = FIRST_WEIGHT * inv_upper
+        second_weight = SECOND_WEIGHT * (inv_upper * inv_upper)
+        weights_out[0:1, :] = jnp.broadcast_to(first_weight, (1, LANES))
+        weights_out[1:2, :] = jnp.broadcast_to(second_weight, (1, LANES))
 
     def write_out(field, target):
         value = field[...]
@@ -668,27 +681,20 @@
         (applied, applied_out),
     ):
         write_out(field, target)
+    sends_done(0)
+    pl.when(is_passing)(pass_done)
+    for wanted, copy in zip(up_to, up):
+        pl.when(wanted)(copy.wait_send)
     pl.when(is_head)(meet_line)
     apply_remote(1, second, applied, local, twice)
     write_out(twice, twice_out)
-    for trade in range(2):
-        for place, target in enumerate(targets):
-            half, g = divmod(place, 4)
-            pl.when(inside(target))(trade_copy(trade, half, g).wait_send)
-    for wanted, copy in zip(up_to, up):
-        pl.when(wanted)(copy.wait_send)
-    pl.when(is_passing)(pass_done)
+    sends_done(1)
     pl.when(is_lookout)(look_out)
     pl.when(jnp.logical_not(jnp.logical_or(is_head, is_lookout)))(down(DOWN)[0].wait_recv)
     for z, chips in RELAY.items():
         pl.when(at_z == z)(functools.partial(start_all, down(chips)))
 
-    inv_upper = 1.0 / jnp.max(top[...], axis=1, keepdims=True)
-    first_weight = FIRST_WEIGHT * inv_upper
-    second_weight = SECOND_WEIGHT * (inv_upper * inv_upper)
-    weights_out[0:1, :] = jnp.broadcast_to(first_weight, (1, LANES))
-    weights_out[1:2, :] = jnp.broadcast_to(second_weight, (1, LANES))
-
+    pl.when(jnp.logical_not(is_head))(write_weights)
     pl.when(is_head)(heads_done)
     for z, chips in RELAY.items():
         pl.when(at_z == z)(functools.partial(wait_all, down(chips)))

time: 28.7 us -> 28.7 us (level)
  no operation moved by 1% of the time
where the time goes in v7:
time: 28.7 us; the launch traced here: 28.4 us
  Pallas kernels  26.2 us (91%)
  between operations  1.32 us (5%)
  other arithmetic  0.77 us (3%)
    pallas_call x1, Pallas kernels, body(): pl.pallas_call(functools.partial(kernel, n), out_shape=[jax.ShapeDtypeStr...  26.2 us
    sub x1, other arithmetic, body(): rhs - weights[0] * applied - weights[1] * twice  0.77 us

profile of v7, /device:TPU:1, one launch (start us, length us, event | category | flops | bytes accessed | tf_op | source)
XLA Modules:
  0.0 28.4 jit_solution(17595985736326370272)
XLA Ops:
  0.6 0.0 copy-start
  1.3 0.0 copy-done
  1.3 26.2 %shard_map.113 = (f32[320,128]{1,0:T(8,128)S(1)}, f32[320,128]{1,0:T(8,128)S(1)}, f32[320,128]{1,0:T(8,128)S(1)}, f32[320,128]{1,0:T(8,128)S(1)}, f32[320,128]{1,0:T(8,128)S(1)}, /*index=5*/f32[2,128]{1,0:T(2,128)S(1)}) custom-call(f32[320,128]{1,0:T(8,128)} %bitcast.15, f32[4,128]{1,0:T(4,128)} %absorption.1, f32[3,128]{1,0:T(4,128)} %geometry.1, ...), custom_call_target="tpu_custom_call" | custom-call | flops 2000000000 | bytes 1000000 | tf_op jit(solution)/shard_map/pallas_call | solution.py:728
  27.6 0.8 %multiply_subtract_fusion = (f32[320,128]{1,0:T(8,128)}, f32[320,128]{1,0:T(8,128)}) fusion(f32[320,128]{1,0:T(8,128)S(1)} %get-tuple-element.13, f32[320,128]{1,0:T(8,128)S(1)} %get-tuple-element.11, f32[320,128]{1,0:T(8,128)S(1)} %get-tuple-element.12, f32[128]{0:T(128)S(1)} %get-tuple-element.17, f32[128]{0:T(128)S(1)} %get-tuple-element.16, ...), kind=kLoop, calls=%fused_computation | loop fusion | flops 286720 | bytes 1147904 | tf_op jit(solution)/shard_map/sub | solution.py:796
  (1 shorter events, 0.0 us)
Async XLA Ops:
  0.6 0.7 %copy-start = (f32[4,128]{1,0:T(4,128)S(1)}, f32[4,128]{1,0:T(4,128)}, u32[]{:S(2)}) copy-start(f32[4,128]{1,0:T(4,128)} %penalty_v.1) | copy-start | bytes 6148
